TPU v7x, 32 devices: a whole 2x2x4 slice. The times are simulated.
32 devices in a mesh: src: 8 (over z, core), rcv: 4 (over y, x).
Axes of the slice: x: 2, y: 2, z: 4, core: 2. Of those that a mesh axis runs over, the one named last changes fastest.
Arguments:
- flows: float32 [24, 1024], P(None, 'src'), may hold values from 0.05 to 2
- speeds: float32 [24, 1024], P(None, 'src'), may hold values from 0.3 to 1.2
- seg_length: float32 [8192], P('src'), may hold values from 10 to 100
- relay_list: int32 [8, 8, 16], P('src'), may hold values from -1 to 127, as said below
- seg_slot: int32 [8192], P('src'), may hold values from 0 to 127, as said below
- tile_pairs: int32 [8, 4, 2, 12], P('src', 'rcv'), may hold values from 0 to 7, as said below
- tile_count: int32 [8, 4], P('src', 'rcv'), may hold values from 2 to 12, as said below
- attenuation: bfloat16 [8, 4, 12, 8, 128, 128], P('src', 'rcv')
- dwellings: int32 [4096], P('rcv'), may hold values from 1 to 22
Outputs:
- grad_flows: float32 [24, 1024], P(None, 'src')
- grad_speeds: float32 [24, 1024], P(None, 'src')
- annoyed_count: float32 [], replicated
Inputs may be any that keep to these rules, and one draw needn't show every extreme that they name: relay_list[d, o, :] holds distinct local link indices of owner o first and -1 after them; from 8 to 16 of them are live, and for every d at least one owner has all 16 live. `seg_slot`: each segment's slot names a live entry of its own block's relay list, and every live entry is named by some segment of that block. `tile_pairs`: entry 0 is a segment block below 8, entry 1 a facade block below 8; the pairs of one device are distinct. Only the first tile_count slots of a device are live; some device has all 12 live.
All inputs are finite; a program needn't handle non-finite values.
Results may differ from a plain program's by a relative error of at most 0.0005.
Values may be sent and summed in bfloat16 or wider, within the bound.
No kernel may reach another device: no remote copies, remote signals or barrier semaphores. Data moves between devices by JAX's collectives and lax.ppermute only.
A program may use at most 64 MiB of HBM per device.

v0:
```python
import functools
import math

import jax
import jax.numpy as jnp
from jax import lax
from jax.experimental import pallas as pl
from jax.experimental.pallas import tpu as pltpu
from jax.sharding import PartitionSpec as P

rolling_base = [79.7, 85.7, 84.5, 90.2, 97.3, 93.9, 84.1, 74.3]
rolling_slope = [30.0, 41.5, 38.9, 25.7, 32.5, 37.2, 39.0, 40.0]
propel_base = [94.5, 89.2, 88.0, 85.9, 84.2, 86.9, 83.3, 76.1]
propel_slope = [-1.3, 7.2, 7.7, 8.0, 8.0, 8.0, 8.0, 8.0]
aweight_db = [-26.2, -16.1, -8.6, -3.2, 0.0, 1.2, 1.0, -1.1]

BANDS = 8
LANES = 128
CLASSES = 3
WIDTH = 16
VMEM_BYTES = 8 * 2**20
ROWS = 4
TOGETHER = 6
ROOT = math.sqrt(10.0)
DECIBEL = math.log(10.0) / 10.0
NT = (((1,), (1,)), ((), ()))


def iota(shape, axis):
    return lax.broadcasted_iota(jnp.int32, shape, axis)


def hour_class(shape):
    hour = iota(shape, 0)
    day = (hour >= 7) & (hour < 19)
    evening = (hour >= 19) & (hour < 23)
    return jnp.where(day, 0, jnp.where(evening, 1, 2))


def band_terms(band, speed_kmh, log_ratio):
    shift = aweight_db[band] - 90.0
    rolling = jnp.exp(
        DECIBEL * (rolling_base[band] + shift) + (DECIBEL * rolling_slope[band]) * log_ratio
    )
    propel = jnp.exp(
        DECIBEL * (propel_base[band] + shift)
        + (DECIBEL * propel_slope[band] / 70.0) * (speed_kmh - 70.0)
    )
    return rolling, propel


def lane_pick(table, index):
    return jnp.take_along_axis(table, index, axis=1, mode="promise_in_bounds")


def swap_groups(block):
    row, lane = iota((8, LANES), 0), iota((8, LANES), 1)
    block = lane_pick(block, (lane + LANES - WIDTH * row) % LANES)
    block = jnp.take_along_axis(
        block, (lane // WIDTH + 8 - row) % 8, axis=0, mode="promise_in_bounds"
    )
    return lane_pick(block, (lane + WIDTH * row) % LANES)


def each_tile(pairs_ref, count, read, multiply, write, acc_ref):
    def step(turn, carry):
        added = []
        for place in range(TOGETHER):
            number = turn * TOGETHER + place
            tile = jnp.minimum(number, count - 1)
            value = read(tile)
            value = jnp.where(number < count, value, jnp.zeros_like(value))
            added.append((write(tile), multiply(value, tile)))
        for block, value in added:
            acc_ref[block] += value
        return carry

    lax.fori_loop(0, (count + TOGETHER - 1) // TOGETHER, step, 0)


def only_band(value, band):
    row = iota(value.shape, 0) % BANDS
    return jnp.where(row == band, value, jnp.zeros_like(value))


def split2(value):
    high = value.astype(jnp.bfloat16)
    low = (value - high.astype(jnp.float32)).astype(jnp.bfloat16)
    return high, low


def source_kernel(copies, flow_hbm, speed_hbm, out_ref, flow_ref, speed_ref, sems):
    fetches = [
        pltpu.make_async_copy(flow_hbm, flow_ref, sems.at[0]),
        pltpu.make_async_copy(speed_hbm, speed_ref, sems.at[1]),
    ]
    for fetch in fetches:
        fetch.start()
    for fetch in fetches:
        fetch.wait()
    flow, speed = flow_ref[...], speed_ref[...]
    kind = hour_class(flow.shape)
    weight = jnp.where(kind == 0, 1.0, jnp.where(kind == 1, ROOT, 10.0))
    speed_kmh = 100.0 * speed
    log_ratio = jnp.log(speed_kmh / 70.0) * (1.0 / math.log(10.0))
    scale = weight * flow / speed_kmh
    row = iota((BANDS, LANES), 0)
    result = jnp.zeros((BANDS, LANES), jnp.float32)
    for band in range(BANDS):
        rolling, propel = band_terms(band, speed_kmh, log_ratio)
        total = jnp.sum(scale * (rolling + propel), axis=0, keepdims=True)
        result = jnp.where(row == band, total, result)
    for copy in range(copies):
        out_ref[copy * BANDS : (copy + 1) * BANDS] = result


def prepare_kernel(
    pairs_hbm, flow_hbm, speed_hbm, slot_hbm, relay_hbm, length_hbm, people_hbm, tile_hbm,
    table_ref, spread_ref, ints_ref, floats_ref, people_ref, tile_ref, pairs_ref, flow_ref, speed_ref, relay_ref, relay_scratch, sems,
):
    owners, blocks = relay_hbm.shape[0], slot_hbm.shape[0]
    index_ref, slot_ref = ints_ref.at[:owners], ints_ref.at[owners:]
    wide_ref, length_ref = floats_ref.at[:owners], floats_ref.at[owners:]
    moves = [
        (flow_hbm, flow_ref),
        (speed_hbm, speed_ref),
        (relay_hbm, relay_ref),
        (slot_hbm, slot_ref),
        (pairs_hbm, pairs_ref),
        (length_hbm, length_ref),
        (people_hbm, people_ref),
        (tile_hbm, tile_ref),
    ]
    fetches = [
        pltpu.make_async_copy(start, end, sems.at[k]) for k, (start, end) in enumerate(moves)
    ]
    for fetch in fetches:
        fetch.start()
    for fetch in fetches[:4]:
        fetch.wait()
    relay_scratch[...] = jnp.zeros(relay_scratch.shape, jnp.int32)
    relay_scratch[:, :WIDTH] = relay_ref[...]
    lane, row = iota((8, LANES), 1), iota((8, LANES), 0)
    for group in range(owners // 8):
        rows = slice(group * 8, group * 8 + 8)
        wide = lane_pick(relay_scratch[rows], lane % WIDTH)
        wide_ref[rows] = wide.astype(jnp.float32)
        picked = jnp.where(lane // WIDTH == row, jnp.maximum(wide, 0), 0)
        picked = jnp.sum(picked, axis=0, keepdims=True)
        index_ref[rows] = jnp.broadcast_to(picked, (8, LANES))
    flow, speed = flow_ref[...], speed_ref[...]
    speed_kmh = 100.0 * speed
    log_ratio = jnp.log(speed_kmh / 70.0) * (1.0 / math.log(10.0))
    per_flow = 1.0 / speed_kmh
    factor = flow * per_flow
    inverse = 1.0 / speed
    for band in range(BANDS):
        rolling, propel = band_terms(band, speed_kmh, log_ratio)
        table_ref[band] = per_flow * (rolling + propel)
        table_ref[BANDS + band] = factor * (
            rolling * (rolling_slope[band] / 10.0 - 1.0) * inverse
            + propel * (math.log(10.0) * propel_slope[band] / 7.0 - inverse)
        )
    slots = spread_ref.shape[1]
    for block in range(blocks):
        same = iota((slots, LANES), 0) == slot_ref[block : block + 1]
        spread_ref[block * LANES : (block + 1) * LANES] = (
            jnp.where(same, 1.0, 0.0).T.astype(jnp.bfloat16)
        )
    for fetch in fetches[4:]:
        fetch.wait()


def turn_kernel(count_ref, tile_ref, part_ref, out_ref):
    def step(tile, carry):
        for band in range(BANDS):
            out_ref[tile, band] = tile_ref[tile, band].T
        return carry

    lax.fori_loop(0, count_ref[0, 0], step, 0)


def forward_kernel(own_blocks, copies, pairs_ref, count_ref, ints_ref, floats_ref, tile_ref, *refs):
    link_refs, (out_ref, seg_scratch, acc_scratch) = refs[:-3], refs[-3:]
    each = link_refs[0].shape[0] // BANDS
    owners = each * len(link_refs)
    groups = owners // 8
    index_ref, slot_ref, length_ref = ints_ref, ints_ref.at[owners:], floats_ref.at[owners:]
    place = iota((BANDS, LANES), 1) // WIDTH
    tables = []
    for group in range(groups):
        index = index_ref[group * 8 : group * 8 + 8]
        table = jnp.zeros((BANDS, LANES), jnp.float32)
        for member in range(8):
            block = group * 8 + member
            rows = slice(block % each * BANDS, (block % each + 1) * BANDS)
            picked = lane_pick(link_refs[block // each][rows], index)
            if own_blocks:
                member = lax.axis_index("src") ^ member
            table = jnp.where(place == member, picked, table)
        tables.append(table)
    blocks = slot_ref.shape[0]
    for block in range(blocks):
        slot = jnp.broadcast_to(slot_ref[block : block + 1], (BANDS, LANES))
        value = lane_pick(tables[0], slot % LANES)
        for group in range(1, groups):
            value = jnp.where(slot // LANES == group, lane_pick(tables[group], slot % LANES), value)
        high, low = split2(value * length_ref[block : block + 1])
        seg_scratch[block] = jnp.concatenate([high, low], axis=0)
    acc_scratch[...] = jnp.zeros(acc_scratch.shape, jnp.float32)

    def multiply(seg, tile):
        rows = jnp.concatenate([only_band(seg, band) for band in range(BANDS)], axis=1)
        tiles = tile_ref[tile].reshape(BANDS * LANES, LANES)
        return jnp.dot(rows, tiles, preferred_element_type=jnp.float32)

    each_tile(
        pairs_ref,
        count_ref[0, 0],
        lambda tile: seg_scratch[pairs_ref[0, tile]],
        multiply,
        lambda tile: pairs_ref[1, tile],
        acc_scratch,
    )
    facades = acc_scratch.shape[0]
    sums = [jnp.sum(acc_scratch[block], axis=0, keepdims=True) for block in range(facades)]
    result = jnp.concatenate(sums, axis=0)
    for copy in range(copies):
        out_ref[copy * facades : (copy + 1) * facades] = result


def backward_kernel(
    hours_weight, receivers, pairs_ref, count_ref, people_ref, floats_ref, spread_ref, tile_ref, *refs
):
    part_refs, (out_ref, grad_scratch, acc_scratch) = refs[:-3], refs[-3:]
    facades = people_ref.shape[0]
    owners = out_ref.shape[0] // (receivers * ROWS)
    relay_ref, length_ref = floats_ref, floats_ref.at[owners:]
    parts = [
        ref[first : first + facades]
        for ref in part_refs
        for first in range(0, ref.shape[0], facades)
    ]
    while len(parts) > 1:
        parts = [sum(parts[k + 1 : k + 2], parts[k]) for k in range(0, len(parts), 2)]
    (total,) = parts
    total = total + 0.01 * hours_weight
    level = 60.0 + (10.0 / math.log(10.0)) * jnp.log(total / 24.0)
    people = people_ref[...].astype(jnp.float32)
    annoyed = people * (78.927 - 3.1162 * level + 0.0342 * level * level) / 100.0
    annoyed = jnp.sum(annoyed, keepdims=True)
    slope = people * (-3.1162 + 0.0684 * level) / 100.0 * (10.0 / math.log(10.0)) / total
    grads = [slope, slope * ROOT, slope * 10.0]
    pad = jnp.zeros((8, LANES), jnp.float32)
    for block in range(facades):
        rows = [jnp.broadcast_to(g[block : block + 1], (BANDS, LANES)) for g in grads]
        grad_scratch[block] = jnp.concatenate(rows + [pad], axis=0).astype(jnp.bfloat16)
    acc_scratch[...] = jnp.zeros(acc_scratch.shape, jnp.float32)

    def multiply(grad, tile):
        rows = jnp.concatenate([only_band(grad, band) for band in range(BANDS)], axis=1)
        tiles = tile_ref[tile].reshape(BANDS * LANES, LANES)
        return jnp.dot(rows, tiles, preferred_element_type=jnp.float32)

    each_tile(
        pairs_ref,
        count_ref[0, 0],
        lambda tile: grad_scratch[pairs_ref[1, tile]],
        multiply,
        lambda tile: pairs_ref[0, tile],
        acc_scratch,
    )
    used = CLASSES * BANDS
    blocks = acc_scratch.shape[0]
    high, low = [], []
    for block in range(blocks):
        value = acc_scratch[block][:used] * length_ref[block : block + 1]
        high_part = value.astype(jnp.bfloat16).astype(jnp.float32)
        high.append(high_part)
        low.append(value - high_part)
    rows = jnp.concatenate(
        [jnp.concatenate(high, axis=1), jnp.concatenate(low, axis=1)], axis=0
    ).astype(jnp.bfloat16)
    slots = jnp.dot(rows, spread_ref[...], preferred_element_type=jnp.float32)
    slots = slots[:used] + slots[used:]
    place = iota((8, LANES), 1) // WIDTH
    for group in range(owners // 8):
        lanes = slice(group * LANES, (group + 1) * LANES)
        rows = [
            swap_groups(slots[kind * BANDS : (kind + 1) * BANDS, lanes])
            for kind in range(CLASSES)
        ]
        rows.append(jnp.where(place == 0, relay_ref[group * 8 : group * 8 + 8], annoyed))
        for receiver in range(receivers):
            first = (receiver * owners + group * 8) * ROWS
            for kind in range(ROWS):
                out_ref[pl.ds(first + kind, 8, stride=ROWS), :] = rows[kind]


def finish_kernel(receivers, in_ref, table_ref, flow_out, speed_out, count_out):
    owners = in_ref.shape[0] // (receivers * ROWS)
    place, row = iota((8, LANES), 1) // WIDTH, iota((8, LANES), 0)
    used = CLASSES * BANDS
    links = jnp.zeros((2 * used, LANES), jnp.float32)
    for group in range(owners // 8):
        parts = []
        for kind in range(ROWS):
            rows = [
                in_ref[pl.ds((receiver * owners + group * 8) * ROWS + kind, 8, stride=ROWS), :]
                for receiver in range(receivers)
            ]
            total = sum(rows[1:], rows[0])
            parts.append(swap_groups(total) if kind < CLASSES else rows[0])
        if group == 0:
            count_out[...] = jnp.broadcast_to(total[0:1, LANES - 1 :], (1, LANES))
        value = jnp.concatenate(parts[:CLASSES], axis=0)
        high = value.astype(jnp.bfloat16).astype(jnp.float32)
        rows = jnp.concatenate([high, value - high], axis=0).astype(jnp.bfloat16)
        relay = lane_pick(parts[CLASSES], iota((8, LANES), 1) % WIDTH)
        relay = jnp.sum(jnp.where(place == row, relay, 0.0), axis=0, keepdims=True)
        relay = relay.astype(jnp.int32)
        spread = jnp.where(iota((LANES, LANES), 0) == relay, 1.0, 0.0).astype(jnp.bfloat16)
        links = links + lax.dot_general(rows, spread, NT, preferred_element_type=jnp.float32)
    links = links[:used] + links[used:]
    kind = hour_class(flow_out.shape)
    flow_sum = jnp.zeros(flow_out.shape, jnp.float32)
    speed_sum = jnp.zeros(flow_out.shape, jnp.float32)
    for band in range(BANDS):
        day, evening, night = [
            links[k * BANDS + band : k * BANDS + band + 1] for k in range(CLASSES)
        ]
        back = jnp.where(kind == 0, day, jnp.where(kind == 1, evening, night))
        flow_sum = flow_sum + back * table_ref[band]
        speed_sum = speed_sum + back * table_ref[BANDS + band]
    flow_out[...] = flow_sum
    speed_out[...] = speed_sum


def call(kernel, name, outs, args, scratch=()):
    space = {"smem": pltpu.SMEM, "vmem": pltpu.VMEM, "hbm": pltpu.HBM}
    return pl.pallas_call(
        kernel,
        out_shape=[
            space[place](shape, dtype) if place else jax.ShapeDtypeStruct(shape, dtype)
            for shape, dtype, place in outs
        ],
        in_specs=[pl.BlockSpec(memory_space=space[place or "smem"]) for _, place in args],
        out_specs=[pl.BlockSpec(memory_space=space[place or "vmem"]) for _, _, place in outs],
        scratch_shapes=list(scratch),
        compiler_params=pltpu.CompilerParams(vmem_limit_bytes=VMEM_BYTES),
        name=name,
    )(
        *[
            pltpu.with_memory_space_constraint(array, space[place]) if place else array
            for array, place in args
        ]
    )


def pair(array, distance):
    sources = lax.axis_size("src")
    return lax.ppermute(array, "src", [(k, k ^ distance) for k in range(sources)])


def shards(
    flows, speeds, seg_length, relay_list, seg_slot, tile_pairs, tile_count, attenuation, dwellings
):
    sources, receivers = lax.axis_size("src"), lax.axis_size("rcv")
    hours = flows.shape[0]
    slots = sources * WIDTH
    f32, i32, bf16 = jnp.float32, jnp.int32, jnp.bfloat16
    blocks, facades = seg_slot.shape[0] // LANES, dwellings.shape[0] // LANES
    hours_weight = sum(
        1.0 if 7 <= h < 19 else (ROOT if 19 <= h < 23 else 10.0) for h in range(hours)
    )

    def vmem(shape, dtype):
        return (shape, dtype, "vmem")

    pairwise = sources == 8
    copies = 1 if pairwise else sources
    (power,) = call(
        functools.partial(source_kernel, copies),
        "source",
        [vmem((copies * BANDS, LANES), f32)],
        [(flows, "hbm"), (speeds, "hbm")],
        [
            pltpu.VMEM((hours, LANES), f32),
            pltpu.VMEM((hours, LANES), f32),
            pltpu.SemaphoreType.DMA((2,)),
        ],
    )
    if pairwise:
        power = jnp.concatenate([power, pair(power, 1)], axis=0)
        powers = [power] + [pair(power, distance) for distance in (2, 4, 6)]
    else:
        powers = [lax.all_to_all(power, "src", 0, 0, tiled=True)]
    tables, spread, ints, floats, people, tiles, pairs = call(
        prepare_kernel,
        "prepare",
        [
            vmem((2 * BANDS, hours, LANES), f32),
            vmem((blocks * LANES, slots), bf16),
            vmem((sources + blocks, LANES), i32),
            vmem((sources + blocks, LANES), f32),
            vmem((facades, LANES), i32),
            vmem(attenuation.shape[2:], bf16),
            (tile_pairs.shape[2:], i32, "smem"),
        ],
        [
            (array, "hbm")
            for array in (
                tile_pairs[0, 0],
                flows,
                speeds,
                seg_slot.reshape(blocks, LANES),
                relay_list[0],
                seg_length.reshape(blocks, LANES),
                dwellings.reshape(facades, LANES),
                attenuation[0, 0],
            )
        ],
        [
            pltpu.VMEM((hours, LANES), f32),
            pltpu.VMEM((hours, LANES), f32),
            pltpu.VMEM((sources, WIDTH), i32),
            pltpu.VMEM((sources, LANES), i32),
            pltpu.SemaphoreType.DMA((8,)),
        ],
    )
    here = [(pairs, "smem"), (tile_count, "")]
    (part,) = call(
        functools.partial(forward_kernel, pairwise, copies),
        "forward",
        [vmem((copies * facades, LANES), f32)],
        here + [(array, "vmem") for array in (ints, floats, tiles, *powers)],
        [
            pltpu.VMEM((blocks, 2 * BANDS, LANES), bf16),
            pltpu.VMEM((facades, 2 * BANDS, LANES), f32),
        ],
    )
    if pairwise:
        total = part + pair(part, 1)
        parts = [total] + [pair(total, distance) for distance in (2, 4, 6)]
    else:
        parts = [lax.all_to_all(part, "src", 0, 0, tiled=True)]
    (turned,) = call(
        turn_kernel,
        "turn",
        [vmem(attenuation.shape[2:], bf16)],
        [(tile_count, ""), (tiles, "vmem"), (part, "vmem")],
    )
    (back,) = call(
        functools.partial(backward_kernel, hours_weight, receivers),
        "backward",
        [vmem((receivers * sources * ROWS, LANES), f32)],
        here + [(array, "vmem") for array in (people, floats, spread, turned, *parts)],
        [
            pltpu.VMEM((facades, 32, LANES), bf16),
            pltpu.VMEM((blocks, 32, LANES), f32),
        ],
    )
    back = back.reshape(receivers * sources, ROWS, LANES)
    back = lax.all_to_all(back, ("rcv", "src"), 0, 0, tiled=True)
    back = back.reshape(receivers * sources * ROWS, LANES)
    grad_flows, grad_speeds, annoyed = call(
        functools.partial(finish_kernel, receivers),
        "finish",
        [((hours, LANES), f32, ""), ((hours, LANES), f32, ""), ((1, LANES), f32, "")],
        [(array, "vmem") for array in (back, tables)],
    )
    return grad_flows, grad_speeds, annoyed[0, 0]


def solution(mesh):
    in_specs = (
        P(None, "src"),
        P(None, "src"),
        P("src"),
        P("src", None, None),
        P("src"),
        P("src", "rcv", None, None),
        P("src", "rcv"),
        P("src", "rcv", None, None, None, None),
        P("rcv"),
    )
    out_specs = (P(None, "src"), P(None, "src"), P())
    return jax.shard_map(shards, mesh=mesh, in_specs=in_specs, out_specs=out_specs, check_vma=False)
```

profile of v0, /device:TPU:0, one launch (start us, length us, event | category | flops | bytes accessed | tf_op | source)
XLA Modules:
  0.0 36.4 jit_solution(17379834071675210698)
XLA Ops:
  0.6 0.8 %source.1 = f32[8,128]{1,0:T(8,128)S(1)} custom-call(f32[24,128]{1,0:T(8,128)} %flow_hbm.3, f32[24,128]{1,0:T(8,128)} %speed_hbm.3), custom_call_target="tpu_custom_call" | custom-call | tf_op jit(solution)/shard_map/source/pallas_call | solution.py:341
  1.4 0.5 %collective-permute-start = (f32[8,128]{1,0:T(8,128)S(1)}, f32[8,128]{1,0:T(8,128)S(1)}, u32[]{:S(2)}, u32[]{:S(2)}) collective-permute-start(f32[8,128]{1,0:T(8,128)S(1)} %source.1), channel_id=1, source_target_pairs={{0,4},{4,0},{8,12},{12,8},{16,20},{20,16},{24,28},{28,24},{1,5},{5... | collective-permute-start | bytes 12296 | tf_op jit(solution)/shard_map/ppermute | solution.py:362
  2.0 0.8 %collective-permute-done = f32[8,128]{1,0:T(8,128)S(1)} collective-permute-done((f32[8,128]{1,0:T(8,128)S(1)}, f32[8,128]{1,0:T(8,128)S(1)}, u32[]{:S(2)}, u32[]{:S(2)}) %collective-permute-start) | collective-permute-done | bytes 4128 | tf_op jit(solution)/shard_map/ppermute | solution.py:362
  2.8 2.9 %collective-permute-start.1 = (f32[16,128]{1,0:T(8,128)S(1)}, f32[16,128]{1,0:T(8,128)S(1)}, u32[]{:S(2)}, u32[]{:S(2)}) collective-permute-start(f32[16,128]{1,0:T(8,128)S(1)} %pad_maximum_fusion.refs_0_), channel_id=1, source_target_pairs={{0,8},{4,12},{8,0},{12,4},{16,24},{20,28},{24,16},{28,20},{1,9},{5... | collective-permute-start | bytes 24584 | tf_op jit(solution)/shard_map/ppermute | solution.py:362
  5.7 2.6 %collective-permute-start.2 = (f32[16,128]{1,0:T(8,128)S(1)}, f32[16,128]{1,0:T(8,128)S(1)}, u32[]{:S(2)}, u32[]{:S(2)}) collective-permute-start(f32[16,128]{1,0:T(8,128)S(1)} %pad_maximum_fusion.refs_0_), channel_id=1, source_target_pairs={{0,16},{4,20},{8,24},{12,28},{16,0},{20,4},{24,8},{28,12},{1,17},{... | collective-permute-start | bytes 24584 | tf_op jit(solution)/shard_map/ppermute | solution.py:362
  8.3 0.0 collective-permute-start.3
  8.9 2.1 %prepare.1 = (f32[16,24,128]{2,1,0:T(8,128)S(1)}, bf16[1024,128]{1,0:T(8,128)(2,1)S(1)}, s32[16,128]{1,0:T(8,128)S(1)}, f32[16,128]{1,0:T(8,128)S(1)}, s32[8,128...) custom-call(s32[2,12]{1,0:T(2,128)} %bitcast.17, f32[24,128]{1,0:T(8,128)} %flow_hbm.3, ...), custom_call_target="tpu_custom_call" | custom-call | tf_op jit(solution)/shard_map/prepare/pallas_call | solution.py:341
  11.0 0.0 collective-permute-done.1.refs_1_
  11.0 0.0 collective-permute-done.2.refs_2_
  11.0 2.7 %collective-permute-done.3.refs_3_ = f32[16,128]{1,0:T(8,128)S(1)} collective-permute-done((f32[16,128]{1,0:T(8,128)S(1)}, f32[16,128]{1,0:T(8,128)S(1)}, u32[]{:S(2)}, u32[]{:S(2)}) %collective-permute-start.3) | collective-permute-done | bytes 8224 | tf_op jit(solution)/shard_map/ppermute | solution.py:362
  13.7 0.5 %forward.1.part_ref = f32[8,128]{1,0:T(8,128)S(1)} custom-call(s32[2,12]{1,0:T(2,128)S(4)} %get-tuple-element.13.pairs_ref, s32[1,1]{1,0:T(1,128)S(6)} %copy.12.count_ref, s32[16,128]{1,0:T(8,128)S(1)} %get-tuple-element.18.ints_ref, f32[16,128]{1,0:T(8,128)S(1)} %get-tuple-element.15.floats_ref, bf16[12,8,128,128]{3,2,1,0:T(8,128)(2,1)S(1)} %get-tuple-element.17.tile_ref, ...), custom_call_target="tpu_custom_call" | custom-call | tf_op jit(solution)/shard_map/forward/pallas_call | solution.py:341
  14.3 0.1 collective-permute-start.4
  14.3 1.2 %collective-permute-done.4 = f32[8,128]{1,0:T(8,128)S(1)} collective-permute-done((f32[8,128]{1,0:T(8,128)S(1)}, f32[8,128]{1,0:T(8,128)S(1)}, u32[]{:S(2)}, u32[]{:S(2)}) %collective-permute-start.4) | collective-permute-done | bytes 4128 | tf_op jit(solution)/shard_map/ppermute | solution.py:362
  15.5 0.0 collective-permute-start.5
  15.5 1.7 %collective-permute-start.6 = (f32[8,128]{1,0:T(8,128)S(1)}, f32[8,128]{1,0:T(8,128)S(1)}, u32[]{:S(2)}, u32[]{:S(2)}) collective-permute-start(f32[8,128]{1,0:T(8,128)S(1)} %add.3.refs_0_), channel_id=1, source_target_pairs={{0,16},{4,20},{8,24},{12,28},{16,0},{20,4},{24,8},{28,12},{1,17},{... | collective-permute-start | bytes 12296 | tf_op jit(solution)/shard_map/ppermute | solution.py:362
  17.2 2.7 %collective-permute-start.7 = (f32[8,128]{1,0:T(8,128)S(1)}, f32[8,128]{1,0:T(8,128)S(1)}, u32[]{:S(2)}, u32[]{:S(2)}) collective-permute-start(f32[8,128]{1,0:T(8,128)S(1)} %add.3.refs_0_), channel_id=1, source_target_pairs={{0,24},{4,28},{8,16},{12,20},{16,8},{20,12},{24,0},{28,4},{1,25},{... | collective-permute-start | bytes 12296 | tf_op jit(solution)/shard_map/ppermute | solution.py:362
  19.9 0.5 %turn.1.tile_ref = bf16[12,8,128,128]{3,2,1,0:T(8,128)(2,1)S(1)} custom-call(s32[1,1]{1,0:T(1,128)S(6)} %copy.12.count_ref, bf16[12,8,128,128]{3,2,1,0:T(8,128)(2,1)S(1)} %get-tuple-element.17.tile_ref, f32[8,128]{1,0:T(8,128)S(1)} %forward.1.part_ref), custom_call_target="tpu_custom_call" | custom-call | tf_op jit(solution)/shard_map/turn/pallas_call | solution.py:341
  20.4 0.0 collective-permute-done.5.refs_1_
  20.4 0.0 collective-permute-done.6.refs_2_
  20.4 2.2 %collective-permute-done.7.refs_3_ = f32[8,128]{1,0:T(8,128)S(1)} collective-permute-done((f32[8,128]{1,0:T(8,128)S(1)}, f32[8,128]{1,0:T(8,128)S(1)}, u32[]{:S(2)}, u32[]{:S(2)}) %collective-permute-start.7) | collective-permute-done | bytes 4128 | tf_op jit(solution)/shard_map/ppermute | solution.py:362
  22.6 0.8 %backward.1 = f32[128,128]{1,0:T(8,128)S(1)} custom-call(s32[2,12]{1,0:T(2,128)S(4)} %get-tuple-element.13.pairs_ref, s32[1,1]{1,0:T(1,128)S(6)} %copy.12.count_ref, s32[8,128]{1,0:T(8,128)S(1)} %get-tuple-element.14.people_ref, f32[16,128]{1,0:T(8,128)S(1)} %get-tuple-element.15.floats_ref, bf16[1024,128]{1,0:T(8,128)(2,1)S(1)} %get-tuple-element.16.spread_ref, ...), custom_call_target="tpu_custom_call" | custom-call | tf_op jit(solution)/shard_map/backward/pallas_call | solution.py:341
  23.4 12.1 %all_to_all.5 = f32[32,4,128]{2,1,0:T(4,128)S(1)} all-to-all(f32[32,4,128]{2,1,0:T(4,128)S(1)} %bitcast.10), channel_id=1, replica_groups=mesh['src'=8,'rcv'=4] {'rcv','src'}, dimensions={0} | all-to-all | bytes 131072 | tf_op jit(solution)/shard_map/all_to_all | solution.py:464
  35.5 0.9 %finish.1 = (f32[24,128]{1,0:T(8,128)}, f32[24,128]{1,0:T(8,128)}, f32[1,128]{1,0:T(1,128)}) custom-call(f32[128,128]{1,0:T(8,128)S(1)} %bitcast.11, f32[16,24,128]{2,1,0:T(8,128)S(1)} %get-tuple-element.19.table_ref), custom_call_target="tpu_custom_call" | custom-call | tf_op jit(solution)/shard_map/finish/pallas_call | solution.py:341
  (2 shorter events, 0.0 us)
Async XLA Ops:
  1.4 1.3 %collective-permute-start = (f32[8,128]{1,0:T(8,128)S(1)}, f32[8,128]{1,0:T(8,128)S(1)}, u32[]{:S(2)}, u32[]{:S(2)}) collective-permute-start(f32[8,128]{1,0:T(8,128)S(1)} %source.1), channel_id=1, source_target_pairs={{0,4},{4,0},{8,12},{12,8},{16,20},{20,16},{24,28},{28,24},{1,5},{5... | collective-permute-start | bytes 12296 | tf_op jit(solution)/shard_map/ppermute | solution.py:362
  2.8 8.2 %collective-permute-start.1 = (f32[16,128]{1,0:T(8,128)S(1)}, f32[16,128]{1,0:T(8,128)S(1)}, u32[]{:S(2)}, u32[]{:S(2)}) collective-permute-start(f32[16,128]{1,0:T(8,128)S(1)} %pad_maximum_fusion.refs_0_), channel_id=1, source_target_pairs={{0,8},{4,12},{8,0},{12,4},{16,24},{20,28},{24,16},{28,20},{1,9},{5... | collective-permute-start | bytes 24584 | tf_op jit(solution)/shard_map/ppermute | solution.py:362
  5.7 5.3 %collective-permute-start.2 = (f32[16,128]{1,0:T(8,128)S(1)}, f32[16,128]{1,0:T(8,128)S(1)}, u32[]{:S(2)}, u32[]{:S(2)}) collective-permute-start(f32[16,128]{1,0:T(8,128)S(1)} %pad_maximum_fusion.refs_0_), channel_id=1, source_target_pairs={{0,16},{4,20},{8,24},{12,28},{16,0},{20,4},{24,8},{28,12},{1,17},{... | collective-permute-start | bytes 24584 | tf_op jit(solution)/shard_map/ppermute | solution.py:362
  8.3 5.4 %collective-permute-start.3 = (f32[16,128]{1,0:T(8,128)S(1)}, f32[16,128]{1,0:T(8,128)S(1)}, u32[]{:S(2)}, u32[]{:S(2)}) collective-permute-start(f32[16,128]{1,0:T(8,128)S(1)} %pad_maximum_fusion.refs_0_), channel_id=1, source_target_pairs={{0,24},{4,28},{8,16},{12,20},{16,8},{20,12},{24,0},{28,4},{1,25},{... | collective-permute-start | bytes 24584 | tf_op jit(solution)/shard_map/ppermute | solution.py:362
  14.3 1.2 %collective-permute-start.4 = (f32[8,128]{1,0:T(8,128)S(1)}, f32[8,128]{1,0:T(8,128)S(1)}, u32[]{:S(2)}, u32[]{:S(2)}) collective-permute-start(f32[8,128]{1,0:T(8,128)S(1)} %forward.1.part_ref), channel_id=1, source_target_pairs={{0,4},{4,0},{8,12},{12,8},{16,20},{20,16},{24,28},{28,24},{1,5},{5... | collective-permute-start | bytes 12296 | tf_op jit(solution)/shard_map/ppermute | solution.py:362
  15.5 4.9 %collective-permute-start.5 = (f32[8,128]{1,0:T(8,128)S(1)}, f32[8,128]{1,0:T(8,128)S(1)}, u32[]{:S(2)}, u32[]{:S(2)}) collective-permute-start(f32[8,128]{1,0:T(8,128)S(1)} %add.3.refs_0_), channel_id=1, source_target_pairs={{0,8},{4,12},{8,0},{12,4},{16,24},{20,28},{24,16},{28,20},{1,9},{5... | collective-permute-start | bytes 12296 | tf_op jit(solution)/shard_map/ppermute | solution.py:362
  15.5 4.9 %collective-permute-start.6 = (f32[8,128]{1,0:T(8,128)S(1)}, f32[8,128]{1,0:T(8,128)S(1)}, u32[]{:S(2)}, u32[]{:S(2)}) collective-permute-start(f32[8,128]{1,0:T(8,128)S(1)} %add.3.refs_0_), channel_id=1, source_target_pairs={{0,16},{4,20},{8,24},{12,28},{16,0},{20,4},{24,8},{28,12},{1,17},{... | collective-permute-start | bytes 12296 | tf_op jit(solution)/shard_map/ppermute | solution.py:362
  17.2 5.4 %collective-permute-start.7 = (f32[8,128]{1,0:T(8,128)S(1)}, f32[8,128]{1,0:T(8,128)S(1)}, u32[]{:S(2)}, u32[]{:S(2)}) collective-permute-start(f32[8,128]{1,0:T(8,128)S(1)} %add.3.refs_0_), channel_id=1, source_target_pairs={{0,24},{4,28},{8,16},{12,20},{16,8},{20,12},{24,0},{28,4},{1,25},{... | collective-permute-start | bytes 12296 | tf_op jit(solution)/shard_map/ppermute | solution.py:362
where the time goes:
time: 37 us; the launch traced here: 36.4 us
  blocking collectives  12.1 us (33%)
  starting transfers between devices  10.5 us (28%)
  waiting for transfers between devices  6.89 us (19%)
  Pallas kernels  5.58 us (15%)
  between operations  1.36 us (4%)
    all_to_all x1, blocking collectives, shards(): back = lax.all_to_all(back, ('rcv', 'src'), 0, 0, tiled=True)  12.1 us
    ppermute x8, starting transfers between devices, pair(): lax.ppermute(array, 'src', [(k, k ^ distance) for k in range(sources)])  10.5 us
    ppermute x8, waiting for transfers between devices, pair(): lax.ppermute(array, 'src', [(k, k ^ distance) for k in range(sources)])  6.89 us
    pallas_call x6, Pallas kernels, call(): pl.pallas_call(kernel, out_shape=[space[place](shape, dtype) if place els...  5.58 us
  transfers between devices with their start and end apart: 8, of which 4 were waited for; matrix products, arithmetic and copies ran while one was open for 0% of the time, Pallas kernels for 7%

commit v1 on v0

--- a/solution.py
+++ b/solution.py
@@ -180,7 +180,7 @@
     lax.fori_loop(0, count_ref[0, 0], step, 0)
 
 
-def forward_kernel(own_blocks, copies, pairs_ref, count_ref, ints_ref, floats_ref, tile_ref, *refs):
+def forward_kernel(distances, copies, pairs_ref, count_ref, ints_ref, floats_ref, tile_ref, *refs):
     link_refs, (out_ref, seg_scratch, acc_scratch) = refs[:-3], refs[-3:]
     each = link_refs[0].shape[0] // BANDS
     owners = each * len(link_refs)
@@ -195,8 +195,8 @@
             block = group * 8 + member
             rows = slice(block % each * BANDS, (block % each + 1) * BANDS)
             picked = lane_pick(link_refs[block // each][rows], index)
-            if own_blocks:
-                member = lax.axis_index("src") ^ member
+            if distances:
+                member = lax.axis_index("src") ^ (distances[block // each] + block % each)
             table = jnp.where(place == member, picked, table)
         tables.append(table)
     blocks = slot_ref.shape[0]
@@ -362,6 +362,14 @@
     return lax.ppermute(array, "src", [(k, k ^ distance) for k in range(sources)])
 
 
+LINKS_ORDER = (4, 6, 2)
+TOTALS_ORDER = (6, 4, 2)
+
+
+def partners(array, distances):
+    return [pair(array, distance) for distance in distances]
+
+
 def shards(
     flows, speeds, seg_length, relay_list, seg_slot, tile_pairs, tile_count, attenuation, dwellings
 ):
@@ -392,7 +400,7 @@
     )
     if pairwise:
         power = jnp.concatenate([power, pair(power, 1)], axis=0)
-        powers = [power] + [pair(power, distance) for distance in (2, 4, 6)]
+        powers = [power] + partners(power, LINKS_ORDER)
     else:
         powers = [lax.all_to_all(power, "src", 0, 0, tiled=True)]
     tables, spread, ints, floats, people, tiles, pairs = call(
@@ -430,7 +438,7 @@
     )
     here = [(pairs, "smem"), (tile_count, "")]
     (part,) = call(
-        functools.partial(forward_kernel, pairwise, copies),
+        functools.partial(forward_kernel, (0, *LINKS_ORDER) if pairwise else (), copies),
         "forward",
         [vmem((copies * facades, LANES), f32)],
         here + [(array, "vmem") for array in (ints, floats, tiles, *powers)],
@@ -441,7 +449,7 @@
     )
     if pairwise:
         total = part + pair(part, 1)
-        parts = [total] + [pair(total, distance) for distance in (2, 4, 6)]
+        parts = [total] + partners(total, TOTALS_ORDER)
     else:
         parts = [lax.all_to_all(part, "src", 0, 0, tiled=True)]
     (turned,) = call(

time: 37 us -> 34.3 us (0.927)
  waiting for transfers between devices: 6.89 us -> 4.76 us
  blocking collectives: 12.1 us -> 11.6 us
    ppermute x8, waiting for transfers between devices: 6.89 us -> 4.76 us  [pair(): lax.ppermute(array, 'src', [(k, k ^ distance) for k in range(sources)])]
    all_to_all x1, blocking collectives: 12.1 us -> 11.6 us  [shards(): back = lax.all_to_all(back, ('rcv', 'src'), 0, 0, tiled=True)]
  transfers between devices with their start and end apart: 8 -> 8, of which waited for: 4 -> 5; matrix products, arithmetic and copies ran while one was open for 0% -> 0% of each run, Pallas kernels for 7% -> 8%
where the time goes in v1:
time: 34.3 us; the launch traced here: 33.7 us
  blocking collectives  11.6 us (34%)
  starting transfers between devices  10.5 us (31%)
  Pallas kernels  5.58 us (16%)
  waiting for transfers between devices  4.76 us (14%)
  between operations  1.34 us (4%)
    all_to_all x1, blocking collectives, shards(): back = lax.all_to_all(back, ('rcv', 'src'), 0, 0, tiled=True)  11.6 us
    ppermute x8, starting transfers between devices, pair(): lax.ppermute(array, 'src', [(k, k ^ distance) for k in range(sources)])  10.5 us
    pallas_call x6, Pallas kernels, call(): pl.pallas_call(kernel, out_shape=[space[place](shape, dtype) if place els...  5.58 us
    ppermute x8, waiting for transfers between devices, pair(): lax.ppermute(array, 'src', [(k, k ^ distance) for k in range(sources)])  4.76 us
  transfers between devices with their start and end apart: 8, of which 5 were waited for; matrix products, arithmetic and copies ran while one was open for 0% of the time, Pallas kernels for 8%

profile of v1, /device:TPU:0, one launch (start us, length us, event | category | flops | bytes accessed | tf_op | source)
XLA Modules:
  0.0 33.7 jit_solution(16461902021351004838)
XLA Ops:
  0.6 0.8 %source.1 = f32[8,128]{1,0:T(8,128)S(1)} custom-call(f32[24,128]{1,0:T(8,128)} %flow_hbm.3, f32[24,128]{1,0:T(8,128)} %speed_hbm.3), custom_call_target="tpu_custom_call" | custom-call | tf_op jit(solution)/shard_map/source/pallas_call | solution.py:341
  1.4 0.5 %collective-permute-start = (f32[8,128]{1,0:T(8,128)S(1)}, f32[8,128]{1,0:T(8,128)S(1)}, u32[]{:S(2)}, u32[]{:S(2)}) collective-permute-start(f32[8,128]{1,0:T(8,128)S(1)} %source.1), channel_id=1, source_target_pairs={{0,4},{4,0},{8,12},{12,8},{16,20},{20,16},{24,28},{28,24},{1,5},{5... | collective-permute-start | bytes 12296 | tf_op jit(solution)/shard_map/ppermute | solution.py:362
  2.0 0.8 %collective-permute-done = f32[8,128]{1,0:T(8,128)S(1)} collective-permute-done((f32[8,128]{1,0:T(8,128)S(1)}, f32[8,128]{1,0:T(8,128)S(1)}, u32[]{:S(2)}, u32[]{:S(2)}) %collective-permute-start) | collective-permute-done | bytes 4128 | tf_op jit(solution)/shard_map/ppermute | solution.py:362
  2.8 3.9 %collective-permute-start.1 = (f32[16,128]{1,0:T(8,128)S(1)}, f32[16,128]{1,0:T(8,128)S(1)}, u32[]{:S(2)}, u32[]{:S(2)}) collective-permute-start(f32[16,128]{1,0:T(8,128)S(1)} %pad_maximum_fusion.refs_0_), channel_id=1, source_target_pairs={{0,16},{4,20},{8,24},{12,28},{16,0},{20,4},{24,8},{28,12},{1,17},{... | collective-permute-start | bytes 24584 | tf_op jit(solution)/shard_map/ppermute | solution.py:362
  6.7 1.3 %collective-permute-start.2 = (f32[16,128]{1,0:T(8,128)S(1)}, f32[16,128]{1,0:T(8,128)S(1)}, u32[]{:S(2)}, u32[]{:S(2)}) collective-permute-start(f32[16,128]{1,0:T(8,128)S(1)} %pad_maximum_fusion.refs_0_), channel_id=1, source_target_pairs={{0,24},{4,28},{8,16},{12,20},{16,8},{20,12},{24,0},{28,4},{1,25},{... | collective-permute-start | bytes 24584 | tf_op jit(solution)/shard_map/ppermute | solution.py:362
  8.1 0.2 collective-permute-start.3
  8.9 2.1 %prepare.1 = (f32[16,24,128]{2,1,0:T(8,128)S(1)}, bf16[1024,128]{1,0:T(8,128)(2,1)S(1)}, s32[16,128]{1,0:T(8,128)S(1)}, f32[16,128]{1,0:T(8,128)S(1)}, s32[8,128...) custom-call(s32[2,12]{1,0:T(2,128)} %bitcast.17, f32[24,128]{1,0:T(8,128)} %flow_hbm.3, ...), custom_call_target="tpu_custom_call" | custom-call | tf_op jit(solution)/shard_map/prepare/pallas_call | solution.py:341
  11.0 0.0 collective-permute-done.1.refs_1_
  11.0 1.1 %collective-permute-done.2.refs_2_ = f32[16,128]{1,0:T(8,128)S(1)} collective-permute-done((f32[16,128]{1,0:T(8,128)S(1)}, f32[16,128]{1,0:T(8,128)S(1)}, u32[]{:S(2)}, u32[]{:S(2)}) %collective-permute-start.2) | collective-permute-done | bytes 8224 | tf_op jit(solution)/shard_map/ppermute | solution.py:362
  12.2 0.0 collective-permute-done.3.refs_3_
  12.2 0.5 %forward.1.part_ref = f32[8,128]{1,0:T(8,128)S(1)} custom-call(s32[2,12]{1,0:T(2,128)S(4)} %get-tuple-element.13.pairs_ref, s32[1,1]{1,0:T(1,128)S(6)} %copy.12.count_ref, s32[16,128]{1,0:T(8,128)S(1)} %get-tuple-element.18.ints_ref, f32[16,128]{1,0:T(8,128)S(1)} %get-tuple-element.15.floats_ref, bf16[12,8,128,128]{3,2,1,0:T(8,128)(2,1)S(1)} %get-tuple-element.17.tile_ref, ...), custom_call_target="tpu_custom_call" | custom-call | tf_op jit(solution)/shard_map/forward/pallas_call | solution.py:341
  12.7 0.1 collective-permute-start.4
  12.8 1.2 %collective-permute-done.4 = f32[8,128]{1,0:T(8,128)S(1)} collective-permute-done((f32[8,128]{1,0:T(8,128)S(1)}, f32[8,128]{1,0:T(8,128)S(1)}, u32[]{:S(2)}, u32[]{:S(2)}) %collective-permute-start.4) | collective-permute-done | bytes 4128 | tf_op jit(solution)/shard_map/ppermute | solution.py:362
  13.9 2.0 %collective-permute-start.5 = (f32[8,128]{1,0:T(8,128)S(1)}, f32[8,128]{1,0:T(8,128)S(1)}, u32[]{:S(2)}, u32[]{:S(2)}) collective-permute-start(f32[8,128]{1,0:T(8,128)S(1)} %add.3.refs_0_), channel_id=1, source_target_pairs={{0,24},{4,28},{8,16},{12,20},{16,8},{20,12},{24,0},{28,4},{1,25},{... | collective-permute-start | bytes 12296 | tf_op jit(solution)/shard_map/ppermute | solution.py:362
  15.9 0.1 collective-permute-start.6
  16.1 2.2 %collective-permute-start.7 = (f32[8,128]{1,0:T(8,128)S(1)}, f32[8,128]{1,0:T(8,128)S(1)}, u32[]{:S(2)}, u32[]{:S(2)}) collective-permute-start(f32[8,128]{1,0:T(8,128)S(1)} %add.3.refs_0_), channel_id=1, source_target_pairs={{0,8},{4,12},{8,0},{12,4},{16,24},{20,28},{24,16},{28,20},{1,9},{5... | collective-permute-start | bytes 12296 | tf_op jit(solution)/shard_map/ppermute | solution.py:362
  18.3 0.5 %turn.1.tile_ref = bf16[12,8,128,128]{3,2,1,0:T(8,128)(2,1)S(1)} custom-call(s32[1,1]{1,0:T(1,128)S(6)} %copy.12.count_ref, bf16[12,8,128,128]{3,2,1,0:T(8,128)(2,1)S(1)} %get-tuple-element.17.tile_ref, f32[8,128]{1,0:T(8,128)S(1)} %forward.1.part_ref), custom_call_target="tpu_custom_call" | custom-call | tf_op jit(solution)/shard_map/turn/pallas_call | solution.py:341
  18.8 0.5 %collective-permute-done.5.refs_1_ = f32[8,128]{1,0:T(8,128)S(1)} collective-permute-done((f32[8,128]{1,0:T(8,128)S(1)}, f32[8,128]{1,0:T(8,128)S(1)}, u32[]{:S(2)}, u32[]{:S(2)}) %collective-permute-start.5) | collective-permute-done | bytes 4128 | tf_op jit(solution)/shard_map/ppermute | solution.py:362
  19.3 1.1 %collective-permute-done.6.refs_2_ = f32[8,128]{1,0:T(8,128)S(1)} collective-permute-done((f32[8,128]{1,0:T(8,128)S(1)}, f32[8,128]{1,0:T(8,128)S(1)}, u32[]{:S(2)}, u32[]{:S(2)}) %collective-permute-start.6) | collective-permute-done | bytes 4128 | tf_op jit(solution)/shard_map/ppermute | solution.py:362
  20.4 0.0 collective-permute-done.7.refs_3_
  20.5 0.8 %backward.1 = f32[128,128]{1,0:T(8,128)S(1)} custom-call(s32[2,12]{1,0:T(2,128)S(4)} %get-tuple-element.13.pairs_ref, s32[1,1]{1,0:T(1,128)S(6)} %copy.12.count_ref, s32[8,128]{1,0:T(8,128)S(1)} %get-tuple-element.14.people_ref, f32[16,128]{1,0:T(8,128)S(1)} %get-tuple-element.15.floats_ref, bf16[1024,128]{1,0:T(8,128)(2,1)S(1)} %get-tuple-element.16.spread_ref, ...), custom_call_target="tpu_custom_call" | custom-call | tf_op jit(solution)/shard_map/backward/pallas_call | solution.py:341
  21.3 11.6 %all_to_all.5 = f32[32,4,128]{2,1,0:T(4,128)S(1)} all-to-all(f32[32,4,128]{2,1,0:T(4,128)S(1)} %bitcast.10), channel_id=1, replica_groups=mesh['src'=8,'rcv'=4] {'rcv','src'}, dimensions={0} | all-to-all | bytes 131072 | tf_op jit(solution)/shard_map/all_to_all | solution.py:472
  32.8 0.9 %finish.1 = (f32[24,128]{1,0:T(8,128)}, f32[24,128]{1,0:T(8,128)}, f32[1,128]{1,0:T(1,128)}) custom-call(f32[128,128]{1,0:T(8,128)S(1)} %bitcast.11, f32[16,24,128]{2,1,0:T(8,128)S(1)} %get-tuple-element.19.table_ref), custom_call_target="tpu_custom_call" | custom-call | tf_op jit(solution)/shard_map/finish/pallas_call | solution.py:341
  (2 shorter events, 0.0 us)
Async XLA Ops:
  1.4 1.3 %collective-permute-start = (f32[8,128]{1,0:T(8,128)S(1)}, f32[8,128]{1,0:T(8,128)S(1)}, u32[]{:S(2)}, u32[]{:S(2)}) collective-permute-start(f32[8,128]{1,0:T(8,128)S(1)} %source.1), channel_id=1, source_target_pairs={{0,4},{4,0},{8,12},{12,8},{16,20},{20,16},{24,28},{28,24},{1,5},{5... | collective-permute-start | bytes 12296 | tf_op jit(solution)/shard_map/ppermute | solution.py:362
  2.8 8.2 %collective-permute-start.1 = (f32[16,128]{1,0:T(8,128)S(1)}, f32[16,128]{1,0:T(8,128)S(1)}, u32[]{:S(2)}, u32[]{:S(2)}) collective-permute-start(f32[16,128]{1,0:T(8,128)S(1)} %pad_maximum_fusion.refs_0_), channel_id=1, source_target_pairs={{0,16},{4,20},{8,24},{12,28},{16,0},{20,4},{24,8},{28,12},{1,17},{... | collective-permute-start | bytes 24584 | tf_op jit(solution)/shard_map/ppermute | solution.py:362
  6.7 5.4 %collective-permute-start.2 = (f32[16,128]{1,0:T(8,128)S(1)}, f32[16,128]{1,0:T(8,128)S(1)}, u32[]{:S(2)}, u32[]{:S(2)}) collective-permute-start(f32[16,128]{1,0:T(8,128)S(1)} %pad_maximum_fusion.refs_0_), channel_id=1, source_target_pairs={{0,24},{4,28},{8,16},{12,20},{16,8},{20,12},{24,0},{28,4},{1,25},{... | collective-permute-start | bytes 24584 | tf_op jit(solution)/shard_map/ppermute | solution.py:362
  8.1 4.1 %collective-permute-start.3 = (f32[16,128]{1,0:T(8,128)S(1)}, f32[16,128]{1,0:T(8,128)S(1)}, u32[]{:S(2)}, u32[]{:S(2)}) collective-permute-start(f32[16,128]{1,0:T(8,128)S(1)} %pad_maximum_fusion.refs_0_), channel_id=1, source_target_pairs={{0,8},{4,12},{8,0},{12,4},{16,24},{20,28},{24,16},{28,20},{1,9},{5... | collective-permute-start | bytes 24584 | tf_op jit(solution)/shard_map/ppermute | solution.py:362
  12.7 1.2 %collective-permute-start.4 = (f32[8,128]{1,0:T(8,128)S(1)}, f32[8,128]{1,0:T(8,128)S(1)}, u32[]{:S(2)}, u32[]{:S(2)}) collective-permute-start(f32[8,128]{1,0:T(8,128)S(1)} %forward.1.part_ref), channel_id=1, source_target_pairs={{0,4},{4,0},{8,12},{12,8},{16,20},{20,16},{24,28},{28,24},{1,5},{5... | collective-permute-start | bytes 12296 | tf_op jit(solution)/shard_map/ppermute | solution.py:362
  13.9 5.4 %collective-permute-start.5 = (f32[8,128]{1,0:T(8,128)S(1)}, f32[8,128]{1,0:T(8,128)S(1)}, u32[]{:S(2)}, u32[]{:S(2)}) collective-permute-start(f32[8,128]{1,0:T(8,128)S(1)} %add.3.refs_0_), channel_id=1, source_target_pairs={{0,24},{4,28},{8,16},{12,20},{16,8},{20,12},{24,0},{28,4},{1,25},{... | collective-permute-start | bytes 12296 | tf_op jit(solution)/shard_map/ppermute | solution.py:362
  15.9 4.5 %collective-permute-start.6 = (f32[8,128]{1,0:T(8,128)S(1)}, f32[8,128]{1,0:T(8,128)S(1)}, u32[]{:S(2)}, u32[]{:S(2)}) collective-permute-start(f32[8,128]{1,0:T(8,128)S(1)} %add.3.refs_0_), channel_id=1, source_target_pairs={{0,16},{4,20},{8,24},{12,28},{16,0},{20,4},{24,8},{28,12},{1,17},{... | collective-permute-start | bytes 12296 | tf_op jit(solution)/shard_map/ppermute | solution.py:362
  16.1 4.4 %collective-permute-start.7 = (f32[8,128]{1,0:T(8,128)S(1)}, f32[8,128]{1,0:T(8,128)S(1)}, u32[]{:S(2)}, u32[]{:S(2)}) collective-permute-start(f32[8,128]{1,0:T(8,128)S(1)} %add.3.refs_0_), channel_id=1, source_target_pairs={{0,8},{4,12},{8,0},{12,4},{16,24},{20,28},{24,16},{28,20},{1,9},{5... | collective-permute-start | bytes 12296 | tf_op jit(solution)/shard_map/ppermute | solution.py:362

commit v2 on v0

--- a/solution.py
+++ b/solution.py
@@ -37,16 +37,22 @@
     return jnp.where(day, 0, jnp.where(evening, 1, 2))
 
 
-def band_terms(band, speed_kmh, log_ratio):
-    shift = aweight_db[band] - 90.0
-    rolling = jnp.exp(
-        DECIBEL * (rolling_base[band] + shift) + (DECIBEL * rolling_slope[band]) * log_ratio
-    )
-    propel = jnp.exp(
-        DECIBEL * (propel_base[band] + shift)
-        + (DECIBEL * propel_slope[band] / 70.0) * (speed_kmh - 70.0)
-    )
-    return rolling, propel
+def log10_ratio(speed_kmh):
+    return jnp.log(speed_kmh / 70.0) * (1.0 / math.log(10.0))
+
+
+def band_terms(speed_kmh, log_ratio):
+    terms, propels = [], {}
+    for band in range(BANDS):
+        shift = aweight_db[band] - 90.0
+        rolling = jnp.exp(
+            DECIBEL * (rolling_base[band] + shift) + (DECIBEL * rolling_slope[band]) * log_ratio
+        )
+        slope = propel_slope[band]
+        if slope not in propels:
+            propels[slope] = jnp.exp((DECIBEL * slope / 70.0) * (speed_kmh - 70.0))
+        terms.append((rolling, math.exp(DECIBEL * (propel_base[band] + shift)) * propels[slope]))
+    return terms
 
 
 def lane_pick(table, index):
@@ -78,6 +84,21 @@
     lax.fori_loop(0, (count + TOGETHER - 1) // TOGETHER, step, 0)
 
 
+def stack_sums(blocks):
+    row = iota((8, LANES), 0)
+    for distance in (4, 2, 1):
+        half = len(blocks) // 2
+        near = (row & distance) == 0
+        blocks = [
+            jnp.where(near, first, second)
+            + jnp.take_along_axis(
+                jnp.where(near, second, first), row ^ distance, axis=0, mode="promise_in_bounds"
+            )
+            for first, second in zip(blocks[:half], blocks[half:])
+        ]
+    return blocks[0]
+
+
 def only_band(value, band):
     row = iota(value.shape, 0) % BANDS
     return jnp.where(row == band, value, jnp.zeros_like(value))
@@ -91,25 +112,25 @@
 
 def source_kernel(copies, flow_hbm, speed_hbm, out_ref, flow_ref, speed_ref, sems):
     fetches = [
-        pltpu.make_async_copy(flow_hbm, flow_ref, sems.at[0]),
-        pltpu.make_async_copy(speed_hbm, speed_ref, sems.at[1]),
+        pltpu.make_async_copy(speed_hbm, speed_ref, sems.at[0]),
+        pltpu.make_async_copy(flow_hbm, flow_ref, sems.at[1]),
     ]
     for fetch in fetches:
         fetch.start()
-    for fetch in fetches:
-        fetch.wait()
-    flow, speed = flow_ref[...], speed_ref[...]
-    kind = hour_class(flow.shape)
-    weight = jnp.where(kind == 0, 1.0, jnp.where(kind == 1, ROOT, 10.0))
+    fetches[0].wait()
+    speed = speed_ref[...]
     speed_kmh = 100.0 * speed
-    log_ratio = jnp.log(speed_kmh / 70.0) * (1.0 / math.log(10.0))
-    scale = weight * flow / speed_kmh
-    row = iota((BANDS, LANES), 0)
-    result = jnp.zeros((BANDS, LANES), jnp.float32)
-    for band in range(BANDS):
-        rolling, propel = band_terms(band, speed_kmh, log_ratio)
-        total = jnp.sum(scale * (rolling + propel), axis=0, keepdims=True)
-        result = jnp.where(row == band, total, result)
+    log_ratio = log10_ratio(speed_kmh)
+    terms = band_terms(speed_kmh, log_ratio)
+    kind = hour_class(speed.shape)
+    weight = jnp.where(kind == 0, 1.0, jnp.where(kind == 1, ROOT, 10.0)) / speed_kmh
+    fetches[1].wait()
+    scale = weight * flow_ref[...]
+    sums = []
+    for rolling, propel in terms:
+        power = scale * (rolling + propel)
+        sums.append(sum(power[k : k + 8] for k in range(8, power.shape[0], 8)) + power[:8])
+    result = stack_sums(sums)
     for copy in range(copies):
         out_ref[copy * BANDS : (copy + 1) * BANDS] = result
 
@@ -150,12 +171,11 @@
         index_ref[rows] = jnp.broadcast_to(picked, (8, LANES))
     flow, speed = flow_ref[...], speed_ref[...]
     speed_kmh = 100.0 * speed
-    log_ratio = jnp.log(speed_kmh / 70.0) * (1.0 / math.log(10.0))
+    terms = band_terms(speed_kmh, log10_ratio(speed_kmh))
     per_flow = 1.0 / speed_kmh
     factor = flow * per_flow
     inverse = 1.0 / speed
-    for band in range(BANDS):
-        rolling, propel = band_terms(band, speed_kmh, log_ratio)
+    for band, (rolling, propel) in enumerate(terms):
         table_ref[band] = per_flow * (rolling + propel)
         table_ref[BANDS + band] = factor * (
             rolling * (rolling_slope[band] / 10.0 - 1.0) * inverse
@@ -180,7 +200,7 @@
     lax.fori_loop(0, count_ref[0, 0], step, 0)
 
 
-def forward_kernel(own_blocks, copies, pairs_ref, count_ref, ints_ref, floats_ref, tile_ref, *refs):
+def forward_kernel(shared, copies, pairs_ref, count_ref, ints_ref, floats_ref, tile_ref, *refs):
     link_refs, (out_ref, seg_scratch, acc_scratch) = refs[:-3], refs[-3:]
     each = link_refs[0].shape[0] // BANDS
     owners = each * len(link_refs)
@@ -195,8 +215,8 @@
             block = group * 8 + member
             rows = slice(block % each * BANDS, (block % each + 1) * BANDS)
             picked = lane_pick(link_refs[block // each][rows], index)
-            if own_blocks:
-                member = lax.axis_index("src") ^ member
+            if shared:
+                member = share_owner(block // each, block % each)
             table = jnp.where(place == member, picked, table)
         tables.append(table)
     blocks = slot_ref.shape[0]
@@ -223,14 +243,13 @@
         acc_scratch,
     )
     facades = acc_scratch.shape[0]
-    sums = [jnp.sum(acc_scratch[block], axis=0, keepdims=True) for block in range(facades)]
-    result = jnp.concatenate(sums, axis=0)
+    result = stack_sums([acc_scratch[block, :8] + acc_scratch[block, 8:] for block in range(facades)])
     for copy in range(copies):
         out_ref[copy * facades : (copy + 1) * facades] = result
 
 
 def backward_kernel(
-    hours_weight, receivers, pairs_ref, count_ref, people_ref, floats_ref, spread_ref, tile_ref, *refs
+    hours, hours_weight, receivers, pairs_ref, count_ref, people_ref, floats_ref, spread_ref, tile_ref, *refs
 ):
     part_refs, (out_ref, grad_scratch, acc_scratch) = refs[:-3], refs[-3:]
     facades = people_ref.shape[0]
@@ -245,11 +264,10 @@
         parts = [sum(parts[k + 1 : k + 2], parts[k]) for k in range(0, len(parts), 2)]
     (total,) = parts
     total = total + 0.01 * hours_weight
-    level = 60.0 + (10.0 / math.log(10.0)) * jnp.log(total / 24.0)
+    level = (60.0 - 10.0 * math.log10(hours)) + (10.0 / math.log(10.0)) * jnp.log(total)
     people = people_ref[...].astype(jnp.float32)
-    annoyed = people * (78.927 - 3.1162 * level + 0.0342 * level * level) / 100.0
-    annoyed = jnp.sum(annoyed, keepdims=True)
-    slope = people * (-3.1162 + 0.0684 * level) / 100.0 * (10.0 / math.log(10.0)) / total
+    rise = (0.1 / math.log(10.0)) * people * (-3.1162 + 0.0684 * level)
+    slope = rise / total
     grads = [slope, slope * ROOT, slope * 10.0]
     pad = jnp.zeros((8, LANES), jnp.float32)
     for block in range(facades):
@@ -270,6 +288,8 @@
         lambda tile: pairs_ref[0, tile],
         acc_scratch,
     )
+    annoyed = (0.01 * people) * (78.927 - 3.1162 * level + 0.0342 * level * level)
+    annoyed = jnp.sum(annoyed, keepdims=True)
     used = CLASSES * BANDS
     blocks = acc_scratch.shape[0]
     high, low = [], []
@@ -357,9 +377,28 @@
     )
 
 
-def pair(array, distance):
+def pair(array, *distances):
     sources = lax.axis_size("src")
-    return lax.ppermute(array, "src", [(k, k ^ distance) for k in range(sources)])
+    return lax.ppermute(
+        array, "src", [(k, k ^ distances[k % len(distances)]) for k in range(sources)]
+    )
+
+
+FAR = (4, 6)
+
+
+def exchange(array, work):
+    far, near = pair(array, *FAR), pair(array, 2)
+    if work:
+        near, far, *work = lax.optimization_barrier((near, far, *work))
+    return [far, pair(far, 1), near, array], work
+
+
+def share_owner(share, member):
+    own = lax.axis_index("src")
+    odd = own % 2
+    first, second = FAR[0] + (FAR[1] - FAR[0]) * odd, FAR[1] + (FAR[0] - FAR[1]) * odd
+    return own ^ (first, second ^ 1, 2, 0)[share] ^ member
 
 
 def shards(
@@ -390,11 +429,6 @@
             pltpu.SemaphoreType.DMA((2,)),
         ],
     )
-    if pairwise:
-        power = jnp.concatenate([power, pair(power, 1)], axis=0)
-        powers = [power] + [pair(power, distance) for distance in (2, 4, 6)]
-    else:
-        powers = [lax.all_to_all(power, "src", 0, 0, tiled=True)]
     tables, spread, ints, floats, people, tiles, pairs = call(
         prepare_kernel,
         "prepare",
@@ -428,6 +462,11 @@
             pltpu.SemaphoreType.DMA((8,)),
         ],
     )
+    if pairwise:
+        power = jnp.concatenate([power, pair(power, 1)], axis=0)
+        powers, (ints,) = exchange(power, [ints])
+    else:
+        powers = [lax.all_to_all(power, "src", 0, 0, tiled=True)]
     here = [(pairs, "smem"), (tile_count, "")]
     (part,) = call(
         functools.partial(forward_kernel, pairwise, copies),
@@ -439,19 +478,19 @@
             pltpu.VMEM((facades, 2 * BANDS, LANES), f32),
         ],
     )
-    if pairwise:
-        total = part + pair(part, 1)
-        parts = [total] + [pair(total, distance) for distance in (2, 4, 6)]
-    else:
-        parts = [lax.all_to_all(part, "src", 0, 0, tiled=True)]
     (turned,) = call(
         turn_kernel,
         "turn",
         [vmem(attenuation.shape[2:], bf16)],
         [(tile_count, ""), (tiles, "vmem"), (part, "vmem")],
     )
+    if pairwise:
+        total = part + pair(part, 1)
+        parts, _ = exchange(total, [])
+    else:
+        parts = [lax.all_to_all(part, "src", 0, 0, tiled=True)]
     (back,) = call(
-        functools.partial(backward_kernel, hours_weight, receivers),
+        functools.partial(backward_kernel, hours, hours_weight, receivers),
         "backward",
         [vmem((receivers * sources * ROWS, LANES), f32)],
         here + [(array, "vmem") for array in (people, floats, spread, turned, *parts)],

time: 37 us -> 32.8 us (0.89)
  starting transfers between devices: 10.5 us -> 8.72 us
  waiting for transfers between devices: 6.89 us -> 5.24 us
  blocking collectives: 12.1 us -> 11.7 us
    ppermute x8, starting transfers between devices: 10.5 us -> 8.72 us  [pair(): lax.ppermute(array, 'src', [(k, k ^ distances[k % len(distances)]) for k...]
    ppermute x8, waiting for transfers between devices: 6.89 us -> 5.24 us  [pair(): lax.ppermute(array, 'src', [(k, k ^ distances[k % len(distances)]) for k...]
    all_to_all x1, blocking collectives: 12.1 us -> 11.7 us  [shards(): back = lax.all_to_all(back, ('rcv', 'src'), 0, 0, tiled=True)]
  transfers between devices with their start and end apart: 8 -> 8, of which waited for: 4 -> 5; matrix products, arithmetic and copies ran while one was open for 0% -> 0% of each run, Pallas kernels for 7% -> 7%
where the time goes in v2:
time: 32.8 us; the launch traced here: 32.4 us
  blocking collectives  11.7 us (36%)
  starting transfers between devices  8.72 us (27%)
  Pallas kernels  5.33 us (16%)
  waiting for transfers between devices  5.24 us (16%)
  between operations  1.34 us (4%)
    all_to_all x1, blocking collectives, shards(): back = lax.all_to_all(back, ('rcv', 'src'), 0, 0, tiled=True)  11.7 us
    ppermute x8, starting transfers between devices, pair(): lax.ppermute(array, 'src', [(k, k ^ distances[k % len(distances)]) for k...  8.72 us
    pallas_call x6, Pallas kernels, call(): pl.pallas_call(kernel, out_shape=[space[place](shape, dtype) if place els...  5.33 us
    ppermute x8, waiting for transfers between devices, pair(): lax.ppermute(array, 'src', [(k, k ^ distances[k % len(distances)]) for k...  5.24 us
  transfers between devices with their start and end apart: 8, of which 5 were waited for; matrix products, arithmetic and copies ran while one was open for 0% of the time, Pallas kernels for 7%

profile of v2, /device:TPU:0, one launch (start us, length us, event | category | flops | bytes accessed | tf_op | source)
XLA Modules:
  0.0 32.4 jit_solution(6870431585425275386)
XLA Ops:
  0.6 0.8 %source.1 = f32[8,128]{1,0:T(8,128)S(1)} custom-call(f32[24,128]{1,0:T(8,128)} %flow_hbm.3, f32[24,128]{1,0:T(8,128)} %speed_hbm.3), custom_call_target="tpu_custom_call" | custom-call | tf_op jit(solution)/shard_map/source/pallas_call | solution.py:361
  1.4 0.5 %collective-permute-start = (f32[8,128]{1,0:T(8,128)S(1)}, f32[8,128]{1,0:T(8,128)S(1)}, u32[]{:S(2)}, u32[]{:S(2)}) collective-permute-start(f32[8,128]{1,0:T(8,128)S(1)} %source.1), channel_id=1, source_target_pairs={{0,4},{4,0},{8,12},{12,8},{16,20},{20,16},{24,28},{28,24},{1,5},{5... | collective-permute-start | bytes 12296 | tf_op jit(solution)/shard_map/ppermute | solution.py:382
  1.9 0.8 %collective-permute-done = f32[8,128]{1,0:T(8,128)S(1)} collective-permute-done((f32[8,128]{1,0:T(8,128)S(1)}, f32[8,128]{1,0:T(8,128)S(1)}, u32[]{:S(2)}, u32[]{:S(2)}) %collective-permute-start) | collective-permute-done | bytes 4128 | tf_op jit(solution)/shard_map/ppermute | solution.py:382
  2.8 3.9 %collective-permute-start.2 = (f32[16,128]{1,0:T(8,128)S(1)}, f32[16,128]{1,0:T(8,128)S(1)}, u32[]{:S(2)}, u32[]{:S(2)}) collective-permute-start(f32[16,128]{1,0:T(8,128)S(1)} %pad_maximum_fusion.refs_3_), channel_id=1, source_target_pairs={{0,16},{4,28},{8,24},{12,20},{16,0},{20,12},{24,8},{28,4},{1,17},{... | collective-permute-start | bytes 24584 | tf_op jit(solution)/shard_map/ppermute | solution.py:382
  6.7 1.6 %collective-permute-start.1 = (f32[16,128]{1,0:T(8,128)S(1)}, f32[16,128]{1,0:T(8,128)S(1)}, u32[]{:S(2)}, u32[]{:S(2)}) collective-permute-start(f32[16,128]{1,0:T(8,128)S(1)} %pad_maximum_fusion.refs_3_), channel_id=1, source_target_pairs={{0,8},{4,12},{8,0},{12,4},{16,24},{20,28},{24,16},{28,20},{1,9},{5... | collective-permute-start | bytes 24584 | tf_op jit(solution)/shard_map/ppermute | solution.py:382
  8.3 2.1 %prepare.1 = (f32[16,24,128]{2,1,0:T(8,128)S(1)}, bf16[1024,128]{1,0:T(8,128)(2,1)S(1)}, s32[16,128]{1,0:T(8,128)S(1)}, f32[16,128]{1,0:T(8,128)S(1)}, s32[8,128...) custom-call(s32[2,12]{1,0:T(2,128)} %bitcast.17, f32[24,128]{1,0:T(8,128)} %flow_hbm.3, ...), custom_call_target="tpu_custom_call" | custom-call | tf_op jit(solution)/shard_map/prepare/pallas_call | solution.py:361
  10.3 0.0 collective-permute-done.2.refs_0_
  10.3 0.0 collective-permute-done.1.refs_2_
  10.4 0.1 collective-permute-start.3
  11.1 0.5 %collective-permute-done.3.refs_1_ = f32[16,128]{1,0:T(8,128)S(1)} collective-permute-done((f32[16,128]{1,0:T(8,128)S(1)}, f32[16,128]{1,0:T(8,128)S(1)}, u32[]{:S(2)}, u32[]{:S(2)}) %collective-permute-start.3) | collective-permute-done | bytes 8224 | tf_op jit(solution)/shard_map/ppermute | solution.py:382
  11.6 0.5 %forward.1.part_ref = f32[8,128]{1,0:T(8,128)S(1)} custom-call(s32[2,12]{1,0:T(2,128)S(4)} %get-tuple-element.16.pairs_ref, s32[1,1]{1,0:T(1,128)S(6)} %copy.12.count_ref, s32[16,128]{1,0:T(8,128)S(1)} %get-tuple-element.22.ints_ref, f32[16,128]{1,0:T(8,128)S(1)} %get-tuple-element.18.floats_ref, bf16[12,8,128,128]{3,2,1,0:T(8,128)(2,1)S(1)} %get-tuple-element.20.tile_ref, ...), custom_call_target="tpu_custom_call" | custom-call | tf_op jit(solution)/shard_map/forward/pallas_call | solution.py:361
  12.1 0.2 collective-permute-start.4
  12.3 1.0 %collective-permute-done.4 = f32[8,128]{1,0:T(8,128)S(1)} collective-permute-done((f32[8,128]{1,0:T(8,128)S(1)}, f32[8,128]{1,0:T(8,128)S(1)}, u32[]{:S(2)}, u32[]{:S(2)}) %collective-permute-start.4) | collective-permute-done | bytes 4128 | tf_op jit(solution)/shard_map/ppermute | solution.py:382
  13.3 0.8 %collective-permute-start.5 = (f32[8,128]{1,0:T(8,128)S(1)}, f32[8,128]{1,0:T(8,128)S(1)}, u32[]{:S(2)}, u32[]{:S(2)}) collective-permute-start(f32[8,128]{1,0:T(8,128)S(1)} %add.3.refs_3_), channel_id=1, source_target_pairs={{0,16},{4,28},{8,24},{12,20},{16,0},{20,12},{24,8},{28,4},{1,17},{... | collective-permute-start | bytes 12296 | tf_op jit(solution)/shard_map/ppermute | solution.py:382
  14.2 1.6 %collective-permute-start.7 = (f32[8,128]{1,0:T(8,128)S(1)}, f32[8,128]{1,0:T(8,128)S(1)}, u32[]{:S(2)}, u32[]{:S(2)}) collective-permute-start(f32[8,128]{1,0:T(8,128)S(1)} %add.3.refs_3_), channel_id=1, source_target_pairs={{0,8},{4,12},{8,0},{12,4},{16,24},{20,28},{24,16},{28,20},{1,9},{5... | collective-permute-start | bytes 12296 | tf_op jit(solution)/shard_map/ppermute | solution.py:382
  15.8 2.1 %collective-permute-done.5.refs_0_ = f32[8,128]{1,0:T(8,128)S(1)} collective-permute-done((f32[8,128]{1,0:T(8,128)S(1)}, f32[8,128]{1,0:T(8,128)S(1)}, u32[]{:S(2)}, u32[]{:S(2)}) %collective-permute-start.5) | collective-permute-done | bytes 4128 | tf_op jit(solution)/shard_map/ppermute | solution.py:382
  17.9 0.0 collective-permute-start.6
  17.9 0.4 %turn.1.tile_ref = bf16[12,8,128,128]{3,2,1,0:T(8,128)(2,1)S(1)} custom-call(s32[1,1]{1,0:T(1,128)S(6)} %copy.12.count_ref, bf16[12,8,128,128]{3,2,1,0:T(8,128)(2,1)S(1)} %get-tuple-element.20.tile_ref, f32[8,128]{1,0:T(8,128)S(1)} %forward.1.part_ref), custom_call_target="tpu_custom_call" | custom-call | tf_op jit(solution)/shard_map/turn/pallas_call | solution.py:361
  18.2 0.0 collective-permute-done.7.refs_2_
  18.2 0.8 %collective-permute-done.6.refs_1_ = f32[8,128]{1,0:T(8,128)S(1)} collective-permute-done((f32[8,128]{1,0:T(8,128)S(1)}, f32[8,128]{1,0:T(8,128)S(1)}, u32[]{:S(2)}, u32[]{:S(2)}) %collective-permute-start.6) | collective-permute-done | bytes 4128 | tf_op jit(solution)/shard_map/ppermute | solution.py:382
  19.0 0.7 %backward.1 = f32[128,128]{1,0:T(8,128)S(1)} custom-call(s32[2,12]{1,0:T(2,128)S(4)} %get-tuple-element.16.pairs_ref, s32[1,1]{1,0:T(1,128)S(6)} %copy.12.count_ref, s32[8,128]{1,0:T(8,128)S(1)} %get-tuple-element.17.people_ref, f32[16,128]{1,0:T(8,128)S(1)} %get-tuple-element.18.floats_ref, bf16[1024,128]{1,0:T(8,128)(2,1)S(1)} %get-tuple-element.19.spread_ref, ...), custom_call_target="tpu_custom_call" | custom-call | tf_op jit(solution)/shard_map/backward/pallas_call | solution.py:361
  19.7 11.7 %all_to_all.5 = f32[32,4,128]{2,1,0:T(4,128)S(1)} all-to-all(f32[32,4,128]{2,1,0:T(4,128)S(1)} %bitcast.10), channel_id=1, replica_groups=mesh['src'=8,'rcv'=4] {'rcv','src'}, dimensions={0} | all-to-all | bytes 131072 | tf_op jit(solution)/shard_map/all_to_all | solution.py:503
  31.5 0.9 %finish.1 = (f32[24,128]{1,0:T(8,128)}, f32[24,128]{1,0:T(8,128)}, f32[1,128]{1,0:T(1,128)}) custom-call(f32[128,128]{1,0:T(8,128)S(1)} %bitcast.11, f32[16,24,128]{2,1,0:T(8,128)S(1)} %get-tuple-element.25.table_ref), custom_call_target="tpu_custom_call" | custom-call | tf_op jit(solution)/shard_map/finish/pallas_call | solution.py:361
  (2 shorter events, 0.0 us)
Async XLA Ops:
  1.4 1.3 %collective-permute-start = (f32[8,128]{1,0:T(8,128)S(1)}, f32[8,128]{1,0:T(8,128)S(1)}, u32[]{:S(2)}, u32[]{:S(2)}) collective-permute-start(f32[8,128]{1,0:T(8,128)S(1)} %source.1), channel_id=1, source_target_pairs={{0,4},{4,0},{8,12},{12,8},{16,20},{20,16},{24,28},{28,24},{1,5},{5... | collective-permute-start | bytes 12296 | tf_op jit(solution)/shard_map/ppermute | solution.py:382
  2.8 7.6 %collective-permute-start.2 = (f32[16,128]{1,0:T(8,128)S(1)}, f32[16,128]{1,0:T(8,128)S(1)}, u32[]{:S(2)}, u32[]{:S(2)}) collective-permute-start(f32[16,128]{1,0:T(8,128)S(1)} %pad_maximum_fusion.refs_3_), channel_id=1, source_target_pairs={{0,16},{4,28},{8,24},{12,20},{16,0},{20,12},{24,8},{28,4},{1,17},{... | collective-permute-start | bytes 24584 | tf_op jit(solution)/shard_map/ppermute | solution.py:382
  6.7 3.7 %collective-permute-start.1 = (f32[16,128]{1,0:T(8,128)S(1)}, f32[16,128]{1,0:T(8,128)S(1)}, u32[]{:S(2)}, u32[]{:S(2)}) collective-permute-start(f32[16,128]{1,0:T(8,128)S(1)} %pad_maximum_fusion.refs_3_), channel_id=1, source_target_pairs={{0,8},{4,12},{8,0},{12,4},{16,24},{20,28},{24,16},{28,20},{1,9},{5... | collective-permute-start | bytes 24584 | tf_op jit(solution)/shard_map/ppermute | solution.py:382
  10.4 1.2 %collective-permute-start.3 = (f32[16,128]{1,0:T(8,128)S(1)}, f32[16,128]{1,0:T(8,128)S(1)}, u32[]{:S(2)}, u32[]{:S(2)}) collective-permute-start(f32[16,128]{1,0:T(8,128)S(1)} %collective-permute-done.2.refs_0_), channel_id=1, source_target_pairs={{0,4},{4,0},{8,12},{12,8},{16,20},{20,16},{24,28},{28,24},{1,5},{5... | collective-permute-start | bytes 24584 | tf_op jit(solution)/shard_map/ppermute | solution.py:382
  12.1 1.2 %collective-permute-start.4 = (f32[8,128]{1,0:T(8,128)S(1)}, f32[8,128]{1,0:T(8,128)S(1)}, u32[]{:S(2)}, u32[]{:S(2)}) collective-permute-start(f32[8,128]{1,0:T(8,128)S(1)} %forward.1.part_ref), channel_id=1, source_target_pairs={{0,4},{4,0},{8,12},{12,8},{16,20},{20,16},{24,28},{28,24},{1,5},{5... | collective-permute-start | bytes 12296 | tf_op jit(solution)/shard_map/ppermute | solution.py:382
  13.3 4.5 %collective-permute-start.5 = (f32[8,128]{1,0:T(8,128)S(1)}, f32[8,128]{1,0:T(8,128)S(1)}, u32[]{:S(2)}, u32[]{:S(2)}) collective-permute-start(f32[8,128]{1,0:T(8,128)S(1)} %add.3.refs_3_), channel_id=1, source_target_pairs={{0,16},{4,28},{8,24},{12,20},{16,0},{20,12},{24,8},{28,4},{1,17},{... | collective-permute-start | bytes 12296 | tf_op jit(solution)/shard_map/ppermute | solution.py:382
  14.2 4.1 %collective-permute-start.7 = (f32[8,128]{1,0:T(8,128)S(1)}, f32[8,128]{1,0:T(8,128)S(1)}, u32[]{:S(2)}, u32[]{:S(2)}) collective-permute-start(f32[8,128]{1,0:T(8,128)S(1)} %add.3.refs_3_), channel_id=1, source_target_pairs={{0,8},{4,12},{8,0},{12,4},{16,24},{20,28},{24,16},{28,20},{1,9},{5... | collective-permute-start | bytes 12296 | tf_op jit(solution)/shard_map/ppermute | solution.py:382
  17.9 1.2 %collective-permute-start.6 = (f32[8,128]{1,0:T(8,128)S(1)}, f32[8,128]{1,0:T(8,128)S(1)}, u32[]{:S(2)}, u32[]{:S(2)}) collective-permute-start(f32[8,128]{1,0:T(8,128)S(1)} %collective-permute-done.5.refs_0_), channel_id=1, source_target_pairs={{0,4},{4,0},{8,12},{12,8},{16,20},{20,16},{24,28},{28,24},{1,5},{5... | collective-permute-start | bytes 12296 | tf_op jit(solution)/shard_map/ppermute | solution.py:382

commit v3 on v2

--- a/solution.py
+++ b/solution.py
@@ -485,7 +485,8 @@
         [(tile_count, ""), (tiles, "vmem"), (part, "vmem")],
     )
     if pairwise:
-        total = part + pair(part, 1)
+        other, turned = lax.optimization_barrier((pair(part, 1), turned))
+        total = part + other
         parts, _ = exchange(total, [])
     else:
         parts = [lax.all_to_all(part, "src", 0, 0, tiled=True)]

time: 32.8 us -> 32.5 us (level)
    all_to_all x1, blocking collectives: 11.7 us -> 11.4 us  [shards(): back = lax.all_to_all(back, ('rcv', 'src'), 0, 0, tiled=True)]
  transfers between devices with their start and end apart: 8 -> 8, of which waited for: 5 -> 6; matrix products, arithmetic and copies ran while one was open for 0% -> 0% of each run, Pallas kernels for 7% -> 7%
where the time goes in v3:
time: 32.5 us; the launch traced here: 32 us
  blocking collectives  11.4 us (35%)
  starting transfers between devices  8.72 us (27%)
  waiting for transfers between devices  5.37 us (17%)
  Pallas kernels  5.21 us (16%)
  between operations  1.33 us (4%)
    all_to_all x1, blocking collectives, shards(): back = lax.all_to_all(back, ('rcv', 'src'), 0, 0, tiled=True)  11.4 us
    ppermute x8, starting transfers between devices, pair(): lax.ppermute(array, 'src', [(k, k ^ distances[k % len(distances)]) for k...  8.72 us
    ppermute x8, waiting for transfers between devices, pair(): lax.ppermute(array, 'src', [(k, k ^ distances[k % len(distances)]) for k...  5.37 us
    pallas_call x6, Pallas kernels, call(): pl.pallas_call(kernel, out_shape=[space[place](shape, dtype) if place els...  5.21 us
  transfers between devices with their start and end apart: 8, of which 6 were waited for; matrix products, arithmetic and copies ran while one was open for 0% of the time, Pallas kernels for 7%

profile of v3, /device:TPU:0, one launch (start us, length us, event | category | flops | bytes accessed | tf_op | source)
XLA Modules:
  0.0 32.0 jit_solution(2347602826809685057)
XLA Ops:
  0.6 0.8 %source.1 = f32[8,128]{1,0:T(8,128)S(1)} custom-call(f32[24,128]{1,0:T(8,128)} %flow_hbm.3, f32[24,128]{1,0:T(8,128)} %speed_hbm.3), custom_call_target="tpu_custom_call" | custom-call | tf_op jit(solution)/shard_map/source/pallas_call | solution.py:361
  1.4 0.5 %collective-permute-start = (f32[8,128]{1,0:T(8,128)S(1)}, f32[8,128]{1,0:T(8,128)S(1)}, u32[]{:S(2)}, u32[]{:S(2)}) collective-permute-start(f32[8,128]{1,0:T(8,128)S(1)} %source.1), channel_id=1, source_target_pairs={{0,4},{4,0},{8,12},{12,8},{16,20},{20,16},{24,28},{28,24},{1,5},{5... | collective-permute-start | bytes 12296 | tf_op jit(solution)/shard_map/ppermute | solution.py:382
  1.9 0.8 %collective-permute-done = f32[8,128]{1,0:T(8,128)S(1)} collective-permute-done((f32[8,128]{1,0:T(8,128)S(1)}, f32[8,128]{1,0:T(8,128)S(1)}, u32[]{:S(2)}, u32[]{:S(2)}) %collective-permute-start) | collective-permute-done | bytes 4128 | tf_op jit(solution)/shard_map/ppermute | solution.py:382
  2.8 3.9 %collective-permute-start.2 = (f32[16,128]{1,0:T(8,128)S(1)}, f32[16,128]{1,0:T(8,128)S(1)}, u32[]{:S(2)}, u32[]{:S(2)}) collective-permute-start(f32[16,128]{1,0:T(8,128)S(1)} %pad_maximum_fusion.refs_3_), channel_id=1, source_target_pairs={{0,16},{4,28},{8,24},{12,20},{16,0},{20,12},{24,8},{28,4},{1,17},{... | collective-permute-start | bytes 24584 | tf_op jit(solution)/shard_map/ppermute | solution.py:382
  6.7 1.6 %collective-permute-start.1 = (f32[16,128]{1,0:T(8,128)S(1)}, f32[16,128]{1,0:T(8,128)S(1)}, u32[]{:S(2)}, u32[]{:S(2)}) collective-permute-start(f32[16,128]{1,0:T(8,128)S(1)} %pad_maximum_fusion.refs_3_), channel_id=1, source_target_pairs={{0,8},{4,12},{8,0},{12,4},{16,24},{20,28},{24,16},{28,20},{1,9},{5... | collective-permute-start | bytes 24584 | tf_op jit(solution)/shard_map/ppermute | solution.py:382
  8.3 2.1 %prepare.1 = (f32[16,24,128]{2,1,0:T(8,128)S(1)}, bf16[1024,128]{1,0:T(8,128)(2,1)S(1)}, s32[16,128]{1,0:T(8,128)S(1)}, f32[16,128]{1,0:T(8,128)S(1)}, s32[8,128...) custom-call(s32[2,12]{1,0:T(2,128)} %bitcast.17, f32[24,128]{1,0:T(8,128)} %flow_hbm.3, ...), custom_call_target="tpu_custom_call" | custom-call | tf_op jit(solution)/shard_map/prepare/pallas_call | solution.py:361
  10.3 0.0 collective-permute-done.2.refs_0_
  10.3 0.0 collective-permute-done.1.refs_2_
  10.4 0.1 collective-permute-start.3
  11.1 0.5 %collective-permute-done.3.refs_1_ = f32[16,128]{1,0:T(8,128)S(1)} collective-permute-done((f32[16,128]{1,0:T(8,128)S(1)}, f32[16,128]{1,0:T(8,128)S(1)}, u32[]{:S(2)}, u32[]{:S(2)}) %collective-permute-start.3) | collective-permute-done | bytes 8224 | tf_op jit(solution)/shard_map/ppermute | solution.py:382
  11.6 0.5 %forward.1.part_ref = f32[8,128]{1,0:T(8,128)S(1)} custom-call(s32[2,12]{1,0:T(2,128)S(4)} %get-tuple-element.18.pairs_ref, s32[1,1]{1,0:T(1,128)S(6)} %copy.12.count_ref, s32[16,128]{1,0:T(8,128)S(1)} %get-tuple-element.23.ints_ref, f32[16,128]{1,0:T(8,128)S(1)} %get-tuple-element.20.floats_ref, bf16[12,8,128,128]{3,2,1,0:T(8,128)(2,1)S(1)} %get-tuple-element.24.tile_ref, ...), custom_call_target="tpu_custom_call" | custom-call | tf_op jit(solution)/shard_map/forward/pallas_call | solution.py:361
  12.1 0.2 collective-permute-start.4
  12.3 0.2 turn.1.tile_ref
  12.6 0.8 %collective-permute-done.4 = f32[8,128]{1,0:T(8,128)S(1)} collective-permute-done((f32[8,128]{1,0:T(8,128)S(1)}, f32[8,128]{1,0:T(8,128)S(1)}, u32[]{:S(2)}, u32[]{:S(2)}) %collective-permute-start.4) | collective-permute-done | bytes 4128 | tf_op jit(solution)/shard_map/ppermute | solution.py:382
  13.3 1.2 %collective-permute-start.5 = (f32[8,128]{1,0:T(8,128)S(1)}, f32[8,128]{1,0:T(8,128)S(1)}, u32[]{:S(2)}, u32[]{:S(2)}) collective-permute-start(f32[8,128]{1,0:T(8,128)S(1)} %add.3.refs_3_), channel_id=1, source_target_pairs={{0,16},{4,28},{8,24},{12,20},{16,0},{20,12},{24,8},{28,4},{1,17},{... | collective-permute-start | bytes 12296 | tf_op jit(solution)/shard_map/ppermute | solution.py:382
  14.5 1.2 %collective-permute-start.7 = (f32[8,128]{1,0:T(8,128)S(1)}, f32[8,128]{1,0:T(8,128)S(1)}, u32[]{:S(2)}, u32[]{:S(2)}) collective-permute-start(f32[8,128]{1,0:T(8,128)S(1)} %add.3.refs_3_), channel_id=1, source_target_pairs={{0,8},{4,12},{8,0},{12,4},{16,24},{20,28},{24,16},{28,20},{1,9},{5... | collective-permute-start | bytes 12296 | tf_op jit(solution)/shard_map/ppermute | solution.py:382
  15.8 2.1 %collective-permute-done.5.refs_0_ = f32[8,128]{1,0:T(8,128)S(1)} collective-permute-done((f32[8,128]{1,0:T(8,128)S(1)}, f32[8,128]{1,0:T(8,128)S(1)}, u32[]{:S(2)}, u32[]{:S(2)}) %collective-permute-start.5) | collective-permute-done | bytes 4128 | tf_op jit(solution)/shard_map/ppermute | solution.py:382
  17.9 0.0 collective-permute-start.6
  17.9 0.3 collective-permute-done.7.refs_2_
  18.2 0.9 %collective-permute-done.6.refs_1_ = f32[8,128]{1,0:T(8,128)S(1)} collective-permute-done((f32[8,128]{1,0:T(8,128)S(1)}, f32[8,128]{1,0:T(8,128)S(1)}, u32[]{:S(2)}, u32[]{:S(2)}) %collective-permute-start.6) | collective-permute-done | bytes 4128 | tf_op jit(solution)/shard_map/ppermute | solution.py:382
  19.0 0.7 %backward.1 = f32[128,128]{1,0:T(8,128)S(1)} custom-call(s32[2,12]{1,0:T(2,128)S(4)} %get-tuple-element.18.pairs_ref, s32[1,1]{1,0:T(1,128)S(6)} %copy.12.count_ref, s32[8,128]{1,0:T(8,128)S(1)} %get-tuple-element.19.people_ref, f32[16,128]{1,0:T(8,128)S(1)} %get-tuple-element.20.floats_ref, bf16[1024,128]{1,0:T(8,128)(2,1)S(1)} %get-tuple-element.21.spread_ref, ...), custom_call_target="tpu_custom_call" | custom-call | tf_op jit(solution)/shard_map/backward/pallas_call | solution.py:361
  19.7 11.4 %all_to_all.5 = f32[32,4,128]{2,1,0:T(4,128)S(1)} all-to-all(f32[32,4,128]{2,1,0:T(4,128)S(1)} %bitcast.10), channel_id=1, replica_groups=mesh['src'=8,'rcv'=4] {'rcv','src'}, dimensions={0} | all-to-all | bytes 131072 | tf_op jit(solution)/shard_map/all_to_all | solution.py:504
  31.1 0.9 %finish.1 = (f32[24,128]{1,0:T(8,128)}, f32[24,128]{1,0:T(8,128)}, f32[1,128]{1,0:T(1,128)}) custom-call(f32[128,128]{1,0:T(8,128)S(1)} %bitcast.11, f32[16,24,128]{2,1,0:T(8,128)S(1)} %get-tuple-element.29.table_ref), custom_call_target="tpu_custom_call" | custom-call | tf_op jit(solution)/shard_map/finish/pallas_call | solution.py:361
  (2 shorter events, 0.0 us)
Async XLA Ops:
  1.4 1.3 %collective-permute-start = (f32[8,128]{1,0:T(8,128)S(1)}, f32[8,128]{1,0:T(8,128)S(1)}, u32[]{:S(2)}, u32[]{:S(2)}) collective-permute-start(f32[8,128]{1,0:T(8,128)S(1)} %source.1), channel_id=1, source_target_pairs={{0,4},{4,0},{8,12},{12,8},{16,20},{20,16},{24,28},{28,24},{1,5},{5... | collective-permute-start | bytes 12296 | tf_op jit(solution)/shard_map/ppermute | solution.py:382
  2.8 7.6 %collective-permute-start.2 = (f32[16,128]{1,0:T(8,128)S(1)}, f32[16,128]{1,0:T(8,128)S(1)}, u32[]{:S(2)}, u32[]{:S(2)}) collective-permute-start(f32[16,128]{1,0:T(8,128)S(1)} %pad_maximum_fusion.refs_3_), channel_id=1, source_target_pairs={{0,16},{4,28},{8,24},{12,20},{16,0},{20,12},{24,8},{28,4},{1,17},{... | collective-permute-start | bytes 24584 | tf_op jit(solution)/shard_map/ppermute | solution.py:382
  6.7 3.7 %collective-permute-start.1 = (f32[16,128]{1,0:T(8,128)S(1)}, f32[16,128]{1,0:T(8,128)S(1)}, u32[]{:S(2)}, u32[]{:S(2)}) collective-permute-start(f32[16,128]{1,0:T(8,128)S(1)} %pad_maximum_fusion.refs_3_), channel_id=1, source_target_pairs={{0,8},{4,12},{8,0},{12,4},{16,24},{20,28},{24,16},{28,20},{1,9},{5... | collective-permute-start | bytes 24584 | tf_op jit(solution)/shard_map/ppermute | solution.py:382
  10.4 1.2 %collective-permute-start.3 = (f32[16,128]{1,0:T(8,128)S(1)}, f32[16,128]{1,0:T(8,128)S(1)}, u32[]{:S(2)}, u32[]{:S(2)}) collective-permute-start(f32[16,128]{1,0:T(8,128)S(1)} %collective-permute-done.2.refs_0_), channel_id=1, source_target_pairs={{0,4},{4,0},{8,12},{12,8},{16,20},{20,16},{24,28},{28,24},{1,5},{5... | collective-permute-start | bytes 24584 | tf_op jit(solution)/shard_map/ppermute | solution.py:382
  12.1 1.2 %collective-permute-start.4 = (f32[8,128]{1,0:T(8,128)S(1)}, f32[8,128]{1,0:T(8,128)S(1)}, u32[]{:S(2)}, u32[]{:S(2)}) collective-permute-start(f32[8,128]{1,0:T(8,128)S(1)} %forward.1.part_ref), channel_id=1, source_target_pairs={{0,4},{4,0},{8,12},{12,8},{16,20},{20,16},{24,28},{28,24},{1,5},{5... | collective-permute-start | bytes 12296 | tf_op jit(solution)/shard_map/ppermute | solution.py:382
  13.3 4.5 %collective-permute-start.5 = (f32[8,128]{1,0:T(8,128)S(1)}, f32[8,128]{1,0:T(8,128)S(1)}, u32[]{:S(2)}, u32[]{:S(2)}) collective-permute-start(f32[8,128]{1,0:T(8,128)S(1)} %add.3.refs_3_), channel_id=1, source_target_pairs={{0,16},{4,28},{8,24},{12,20},{16,0},{20,12},{24,8},{28,4},{1,17},{... | collective-permute-start | bytes 12296 | tf_op jit(solution)/shard_map/ppermute | solution.py:382
  14.5 3.6 %collective-permute-start.7 = (f32[8,128]{1,0:T(8,128)S(1)}, f32[8,128]{1,0:T(8,128)S(1)}, u32[]{:S(2)}, u32[]{:S(2)}) collective-permute-start(f32[8,128]{1,0:T(8,128)S(1)} %add.3.refs_3_), channel_id=1, source_target_pairs={{0,8},{4,12},{8,0},{12,4},{16,24},{20,28},{24,16},{28,20},{1,9},{5... | collective-permute-start | bytes 12296 | tf_op jit(solution)/shard_map/ppermute | solution.py:382
  17.9 1.2 %collective-permute-start.6 = (f32[8,128]{1,0:T(8,128)S(1)}, f32[8,128]{1,0:T(8,128)S(1)}, u32[]{:S(2)}, u32[]{:S(2)}) collective-permute-start(f32[8,128]{1,0:T(8,128)S(1)} %collective-permute-done.5.refs_0_), channel_id=1, source_target_pairs={{0,4},{4,0},{8,12},{12,8},{16,20},{20,16},{24,28},{28,24},{1,5},{5... | collective-permute-start | bytes 12296 | tf_op jit(solution)/shard_map/ppermute | solution.py:382

commit v4 on v3

--- a/solution.py
+++ b/solution.py
@@ -21,6 +21,7 @@
 VMEM_BYTES = 8 * 2**20
 ROWS = 4
 TOGETHER = 6
+TURNED = 4
 ROOT = math.sqrt(10.0)
 DECIBEL = math.log(10.0) / 10.0
 NT = (((1,), (1,)), ((), ()))
@@ -192,12 +193,16 @@
 
 
 def turn_kernel(count_ref, tile_ref, part_ref, out_ref):
-    def step(tile, carry):
-        for band in range(BANDS):
-            out_ref[tile, band] = tile_ref[tile, band].T
+    count = count_ref[0, 0]
+
+    def step(turn, carry):
+        for place in range(TURNED):
+            tile = jnp.minimum(turn * TURNED + place, count - 1)
+            for band in range(BANDS):
+                out_ref[tile, band] = tile_ref[tile, band].T
         return carry
 
-    lax.fori_loop(0, count_ref[0, 0], step, 0)
+    lax.fori_loop(0, (count + TURNED - 1) // TURNED, step, 0)
 
 
 def forward_kernel(shared, copies, pairs_ref, count_ref, ints_ref, floats_ref, tile_ref, *refs):

time: 32.5 us -> 32.4 us (level)
  waiting for transfers between devices: 5.37 us -> 4.96 us
  starting transfers between devices: 8.72 us -> 9.05 us
    ppermute x8, waiting for transfers between devices: 5.37 us -> 4.96 us  [pair(): lax.ppermute(array, 'src', [(k, k ^ distances[k % len(distances)]) for k...]
    ppermute x8, starting transfers between devices: 8.72 us -> 9.05 us  [pair(): lax.ppermute(array, 'src', [(k, k ^ distances[k % len(distances)]) for k...]
where the time goes in v4:
time: 32.4 us; the launch traced here: 32 us
  blocking collectives  11.4 us (35%)
  starting transfers between devices  9.05 us (28%)
  Pallas kernels  5.29 us (16%)
  waiting for transfers between devices  4.96 us (15%)
  between operations  1.33 us (4%)
    all_to_all x1, blocking collectives, shards(): back = lax.all_to_all(back, ('rcv', 'src'), 0, 0, tiled=True)  11.4 us
    ppermute x8, starting transfers between devices, pair(): lax.ppermute(array, 'src', [(k, k ^ distances[k % len(distances)]) for k...  9.05 us
    pallas_call x6, Pallas kernels, call(): pl.pallas_call(kernel, out_shape=[space[place](shape, dtype) if place els...  5.29 us
    ppermute x8, waiting for transfers between devices, pair(): lax.ppermute(array, 'src', [(k, k ^ distances[k % len(distances)]) for k...  4.96 us
  transfers between devices with their start and end apart: 8, of which 6 were waited for; matrix products, arithmetic and copies ran while one was open for 0% of the time, Pallas kernels for 7%

profile of v4, /device:TPU:0, one launch (start us, length us, event | category | flops | bytes accessed | tf_op | source)
XLA Modules:
  0.0 32.0 jit_solution(8393498669718751247)
XLA Ops:
  0.6 0.8 %source.1 = f32[8,128]{1,0:T(8,128)S(1)} custom-call(f32[24,128]{1,0:T(8,128)} %flow_hbm.3, f32[24,128]{1,0:T(8,128)} %speed_hbm.3), custom_call_target="tpu_custom_call" | custom-call | tf_op jit(solution)/shard_map/source/pallas_call | solution.py:366
  1.4 0.5 %collective-permute-start = (f32[8,128]{1,0:T(8,128)S(1)}, f32[8,128]{1,0:T(8,128)S(1)}, u32[]{:S(2)}, u32[]{:S(2)}) collective-permute-start(f32[8,128]{1,0:T(8,128)S(1)} %source.1), channel_id=1, source_target_pairs={{0,4},{4,0},{8,12},{12,8},{16,20},{20,16},{24,28},{28,24},{1,5},{5... | collective-permute-start | bytes 12296 | tf_op jit(solution)/shard_map/ppermute | solution.py:387
  1.9 0.8 %collective-permute-done = f32[8,128]{1,0:T(8,128)S(1)} collective-permute-done((f32[8,128]{1,0:T(8,128)S(1)}, f32[8,128]{1,0:T(8,128)S(1)}, u32[]{:S(2)}, u32[]{:S(2)}) %collective-permute-start) | collective-permute-done | bytes 4128 | tf_op jit(solution)/shard_map/ppermute | solution.py:387
  2.8 3.9 %collective-permute-start.2 = (f32[16,128]{1,0:T(8,128)S(1)}, f32[16,128]{1,0:T(8,128)S(1)}, u32[]{:S(2)}, u32[]{:S(2)}) collective-permute-start(f32[16,128]{1,0:T(8,128)S(1)} %pad_maximum_fusion.refs_3_), channel_id=1, source_target_pairs={{0,16},{4,28},{8,24},{12,20},{16,0},{20,12},{24,8},{28,4},{1,17},{... | collective-permute-start | bytes 24584 | tf_op jit(solution)/shard_map/ppermute | solution.py:387
  6.7 1.6 %collective-permute-start.1 = (f32[16,128]{1,0:T(8,128)S(1)}, f32[16,128]{1,0:T(8,128)S(1)}, u32[]{:S(2)}, u32[]{:S(2)}) collective-permute-start(f32[16,128]{1,0:T(8,128)S(1)} %pad_maximum_fusion.refs_3_), channel_id=1, source_target_pairs={{0,8},{4,12},{8,0},{12,4},{16,24},{20,28},{24,16},{28,20},{1,9},{5... | collective-permute-start | bytes 24584 | tf_op jit(solution)/shard_map/ppermute | solution.py:387
  8.3 2.1 %prepare.1 = (f32[16,24,128]{2,1,0:T(8,128)S(1)}, bf16[1024,128]{1,0:T(8,128)(2,1)S(1)}, s32[16,128]{1,0:T(8,128)S(1)}, f32[16,128]{1,0:T(8,128)S(1)}, s32[8,128...) custom-call(s32[2,12]{1,0:T(2,128)} %bitcast.17, f32[24,128]{1,0:T(8,128)} %flow_hbm.3, ...), custom_call_target="tpu_custom_call" | custom-call | tf_op jit(solution)/shard_map/prepare/pallas_call | solution.py:366
  10.3 0.0 collective-permute-done.2.refs_0_
  10.3 0.0 collective-permute-done.1.refs_2_
  10.4 0.1 collective-permute-start.3
  11.1 0.5 %collective-permute-done.3.refs_1_ = f32[16,128]{1,0:T(8,128)S(1)} collective-permute-done((f32[16,128]{1,0:T(8,128)S(1)}, f32[16,128]{1,0:T(8,128)S(1)}, u32[]{:S(2)}, u32[]{:S(2)}) %collective-permute-start.3) | collective-permute-done | bytes 8224 | tf_op jit(solution)/shard_map/ppermute | solution.py:387
  11.6 0.5 %forward.1.part_ref = f32[8,128]{1,0:T(8,128)S(1)} custom-call(s32[2,12]{1,0:T(2,128)S(4)} %get-tuple-element.18.pairs_ref, s32[1,1]{1,0:T(1,128)S(6)} %copy.12.count_ref, s32[16,128]{1,0:T(8,128)S(1)} %get-tuple-element.23.ints_ref, f32[16,128]{1,0:T(8,128)S(1)} %get-tuple-element.20.floats_ref, bf16[12,8,128,128]{3,2,1,0:T(8,128)(2,1)S(1)} %get-tuple-element.24.tile_ref, ...), custom_call_target="tpu_custom_call" | custom-call | tf_op jit(solution)/shard_map/forward/pallas_call | solution.py:366
  12.1 0.2 collective-permute-start.4
  12.3 0.3 %turn.1.tile_ref = bf16[12,8,128,128]{3,2,1,0:T(8,128)(2,1)S(1)} custom-call(s32[1,1]{1,0:T(1,128)S(6)} %copy.12.count_ref, bf16[12,8,128,128]{3,2,1,0:T(8,128)(2,1)S(1)} %get-tuple-element.24.tile_ref, f32[8,128]{1,0:T(8,128)S(1)} %forward.1.part_ref), custom_call_target="tpu_custom_call" | custom-call | tf_op jit(solution)/shard_map/turn/pallas_call | solution.py:366
  12.7 0.7 %collective-permute-done.4 = f32[8,128]{1,0:T(8,128)S(1)} collective-permute-done((f32[8,128]{1,0:T(8,128)S(1)}, f32[8,128]{1,0:T(8,128)S(1)}, u32[]{:S(2)}, u32[]{:S(2)}) %collective-permute-start.4) | collective-permute-done | bytes 4128 | tf_op jit(solution)/shard_map/ppermute | solution.py:387
  13.3 1.2 %collective-permute-start.5 = (f32[8,128]{1,0:T(8,128)S(1)}, f32[8,128]{1,0:T(8,128)S(1)}, u32[]{:S(2)}, u32[]{:S(2)}) collective-permute-start(f32[8,128]{1,0:T(8,128)S(1)} %add.3.refs_3_), channel_id=1, source_target_pairs={{0,16},{4,28},{8,24},{12,20},{16,0},{20,12},{24,8},{28,4},{1,17},{... | collective-permute-start | bytes 12296 | tf_op jit(solution)/shard_map/ppermute | solution.py:387
  14.5 1.6 %collective-permute-start.7 = (f32[8,128]{1,0:T(8,128)S(1)}, f32[8,128]{1,0:T(8,128)S(1)}, u32[]{:S(2)}, u32[]{:S(2)}) collective-permute-start(f32[8,128]{1,0:T(8,128)S(1)} %add.3.refs_3_), channel_id=1, source_target_pairs={{0,8},{4,12},{8,0},{12,4},{16,24},{20,28},{24,16},{28,20},{1,9},{5... | collective-permute-start | bytes 12296 | tf_op jit(solution)/shard_map/ppermute | solution.py:387
  16.1 1.8 %collective-permute-done.5.refs_0_ = f32[8,128]{1,0:T(8,128)S(1)} collective-permute-done((f32[8,128]{1,0:T(8,128)S(1)}, f32[8,128]{1,0:T(8,128)S(1)}, u32[]{:S(2)}, u32[]{:S(2)}) %collective-permute-start.5) | collective-permute-done | bytes 4128 | tf_op jit(solution)/shard_map/ppermute | solution.py:387
  17.9 0.0 collective-permute-start.6
  17.9 0.3 collective-permute-done.7.refs_2_
  18.1 0.9 %collective-permute-done.6.refs_1_ = f32[8,128]{1,0:T(8,128)S(1)} collective-permute-done((f32[8,128]{1,0:T(8,128)S(1)}, f32[8,128]{1,0:T(8,128)S(1)}, u32[]{:S(2)}, u32[]{:S(2)}) %collective-permute-start.6) | collective-permute-done | bytes 4128 | tf_op jit(solution)/shard_map/ppermute | solution.py:387
  19.0 0.7 %backward.1 = f32[128,128]{1,0:T(8,128)S(1)} custom-call(s32[2,12]{1,0:T(2,128)S(4)} %get-tuple-element.18.pairs_ref, s32[1,1]{1,0:T(1,128)S(6)} %copy.12.count_ref, s32[8,128]{1,0:T(8,128)S(1)} %get-tuple-element.19.people_ref, f32[16,128]{1,0:T(8,128)S(1)} %get-tuple-element.20.floats_ref, bf16[1024,128]{1,0:T(8,128)(2,1)S(1)} %get-tuple-element.21.spread_ref, ...), custom_call_target="tpu_custom_call" | custom-call | tf_op jit(solution)/shard_map/backward/pallas_call | solution.py:366
  19.7 11.4 %all_to_all.5 = f32[32,4,128]{2,1,0:T(4,128)S(1)} all-to-all(f32[32,4,128]{2,1,0:T(4,128)S(1)} %bitcast.10), channel_id=1, replica_groups=mesh['src'=8,'rcv'=4] {'rcv','src'}, dimensions={0} | all-to-all | bytes 131072 | tf_op jit(solution)/shard_map/all_to_all | solution.py:509
  31.1 0.9 %finish.1 = (f32[24,128]{1,0:T(8,128)}, f32[24,128]{1,0:T(8,128)}, f32[1,128]{1,0:T(1,128)}) custom-call(f32[128,128]{1,0:T(8,128)S(1)} %bitcast.11, f32[16,24,128]{2,1,0:T(8,128)S(1)} %get-tuple-element.29.table_ref), custom_call_target="tpu_custom_call" | custom-call | tf_op jit(solution)/shard_map/finish/pallas_call | solution.py:366
  (2 shorter events, 0.0 us)
Async XLA Ops:
  1.4 1.3 %collective-permute-start = (f32[8,128]{1,0:T(8,128)S(1)}, f32[8,128]{1,0:T(8,128)S(1)}, u32[]{:S(2)}, u32[]{:S(2)}) collective-permute-start(f32[8,128]{1,0:T(8,128)S(1)} %source.1), channel_id=1, source_target_pairs={{0,4},{4,0},{8,12},{12,8},{16,20},{20,16},{24,28},{28,24},{1,5},{5... | collective-permute-start | bytes 12296 | tf_op jit(solution)/shard_map/ppermute | solution.py:387
  2.8 7.6 %collective-permute-start.2 = (f32[16,128]{1,0:T(8,128)S(1)}, f32[16,128]{1,0:T(8,128)S(1)}, u32[]{:S(2)}, u32[]{:S(2)}) collective-permute-start(f32[16,128]{1,0:T(8,128)S(1)} %pad_maximum_fusion.refs_3_), channel_id=1, source_target_pairs={{0,16},{4,28},{8,24},{12,20},{16,0},{20,12},{24,8},{28,4},{1,17},{... | collective-permute-start | bytes 24584 | tf_op jit(solution)/shard_map/ppermute | solution.py:387
  6.7 3.7 %collective-permute-start.1 = (f32[16,128]{1,0:T(8,128)S(1)}, f32[16,128]{1,0:T(8,128)S(1)}, u32[]{:S(2)}, u32[]{:S(2)}) collective-permute-start(f32[16,128]{1,0:T(8,128)S(1)} %pad_maximum_fusion.refs_3_), channel_id=1, source_target_pairs={{0,8},{4,12},{8,0},{12,4},{16,24},{20,28},{24,16},{28,20},{1,9},{5... | collective-permute-start | bytes 24584 | tf_op jit(solution)/shard_map/ppermute | solution.py:387
  10.4 1.2 %collective-permute-start.3 = (f32[16,128]{1,0:T(8,128)S(1)}, f32[16,128]{1,0:T(8,128)S(1)}, u32[]{:S(2)}, u32[]{:S(2)}) collective-permute-start(f32[16,128]{1,0:T(8,128)S(1)} %collective-permute-done.2.refs_0_), channel_id=1, source_target_pairs={{0,4},{4,0},{8,12},{12,8},{16,20},{20,16},{24,28},{28,24},{1,5},{5... | collective-permute-start | bytes 24584 | tf_op jit(solution)/shard_map/ppermute | solution.py:387
  12.1 1.2 %collective-permute-start.4 = (f32[8,128]{1,0:T(8,128)S(1)}, f32[8,128]{1,0:T(8,128)S(1)}, u32[]{:S(2)}, u32[]{:S(2)}) collective-permute-start(f32[8,128]{1,0:T(8,128)S(1)} %forward.1.part_ref), channel_id=1, source_target_pairs={{0,4},{4,0},{8,12},{12,8},{16,20},{20,16},{24,28},{28,24},{1,5},{5... | collective-permute-start | bytes 12296 | tf_op jit(solution)/shard_map/ppermute | solution.py:387
  13.3 4.5 %collective-permute-start.5 = (f32[8,128]{1,0:T(8,128)S(1)}, f32[8,128]{1,0:T(8,128)S(1)}, u32[]{:S(2)}, u32[]{:S(2)}) collective-permute-start(f32[8,128]{1,0:T(8,128)S(1)} %add.3.refs_3_), channel_id=1, source_target_pairs={{0,16},{4,28},{8,24},{12,20},{16,0},{20,12},{24,8},{28,4},{1,17},{... | collective-permute-start | bytes 12296 | tf_op jit(solution)/shard_map/ppermute | solution.py:387
  14.5 3.6 %collective-permute-start.7 = (f32[8,128]{1,0:T(8,128)S(1)}, f32[8,128]{1,0:T(8,128)S(1)}, u32[]{:S(2)}, u32[]{:S(2)}) collective-permute-start(f32[8,128]{1,0:T(8,128)S(1)} %add.3.refs_3_), channel_id=1, source_target_pairs={{0,8},{4,12},{8,0},{12,4},{16,24},{20,28},{24,16},{28,20},{1,9},{5... | collective-permute-start | bytes 12296 | tf_op jit(solution)/shard_map/ppermute | solution.py:387
  17.9 1.2 %collective-permute-start.6 = (f32[8,128]{1,0:T(8,128)S(1)}, f32[8,128]{1,0:T(8,128)S(1)}, u32[]{:S(2)}, u32[]{:S(2)}) collective-permute-start(f32[8,128]{1,0:T(8,128)S(1)} %collective-permute-done.5.refs_0_), channel_id=1, source_target_pairs={{0,4},{4,0},{8,12},{12,8},{16,20},{20,16},{24,28},{28,24},{1,5},{5... | collective-permute-start | bytes 12296 | tf_op jit(solution)/shard_map/ppermute | solution.py:387

commit v5 on v4

--- a/solution.py
+++ b/solution.py
@@ -21,7 +21,7 @@
 VMEM_BYTES = 8 * 2**20
 ROWS = 4
 TOGETHER = 6
-TURNED = 4
+TURNED = 3
 ROOT = math.sqrt(10.0)
 DECIBEL = math.log(10.0) / 10.0
 NT = (((1,), (1,)), ((), ()))
@@ -156,7 +156,7 @@
     fetches = [
         pltpu.make_async_copy(start, end, sems.at[k]) for k, (start, end) in enumerate(moves)
     ]
-    for fetch in fetches:
+    for fetch in fetches[:4] + fetches[-1:] + fetches[4:-1]:
         fetch.start()
     for fetch in fetches[:4]:
         fetch.wait()

time: 32.4 us -> 32.5 us (level)
  transfers between devices with their start and end apart: 8 -> 8, of which waited for: 6 -> 5; matrix products, arithmetic and copies ran while one was open for 0% -> 0% of each run, Pallas kernels for 7% -> 7%
where the time goes in v5:
time: 32.5 us; the launch traced here: 31.9 us
  blocking collectives  11.3 us (35%)
  starting transfers between devices  8.89 us (27%)
  waiting for transfers between devices  5.2 us (16%)
  Pallas kernels  5.19 us (16%)
  between operations  1.33 us (4%)
    all_to_all x1, blocking collectives, shards(): back = lax.all_to_all(back, ('rcv', 'src'), 0, 0, tiled=True)  11.3 us
    ppermute x8, starting transfers between devices, pair(): lax.ppermute(array, 'src', [(k, k ^ distances[k % len(distances)]) for k...  8.89 us
    ppermute x8, waiting for transfers between devices, pair(): lax.ppermute(array, 'src', [(k, k ^ distances[k % len(distances)]) for k...  5.2 us
    pallas_call x6, Pallas kernels, call(): pl.pallas_call(kernel, out_shape=[space[place](shape, dtype) if place els...  5.19 us
  transfers between devices with their start and end apart: 8, of which 5 were waited for; matrix products, arithmetic and copies ran while one was open for 0% of the time, Pallas kernels for 7%

profile of v5, /device:TPU:0, one launch (start us, length us, event | category | flops | bytes accessed | tf_op | source)
XLA Modules:
  0.0 31.9 jit_solution(4508038836182163797)
XLA Ops:
  0.6 0.8 %source.1 = f32[8,128]{1,0:T(8,128)S(1)} custom-call(f32[24,128]{1,0:T(8,128)} %flow_hbm.3, f32[24,128]{1,0:T(8,128)} %speed_hbm.3), custom_call_target="tpu_custom_call" | custom-call | tf_op jit(solution)/shard_map/source/pallas_call | solution.py:366
  1.4 0.5 %collective-permute-start = (f32[8,128]{1,0:T(8,128)S(1)}, f32[8,128]{1,0:T(8,128)S(1)}, u32[]{:S(2)}, u32[]{:S(2)}) collective-permute-start(f32[8,128]{1,0:T(8,128)S(1)} %source.1), channel_id=1, source_target_pairs={{0,4},{4,0},{8,12},{12,8},{16,20},{20,16},{24,28},{28,24},{1,5},{5... | collective-permute-start | bytes 12296 | tf_op jit(solution)/shard_map/ppermute | solution.py:387
  1.9 0.8 %collective-permute-done = f32[8,128]{1,0:T(8,128)S(1)} collective-permute-done((f32[8,128]{1,0:T(8,128)S(1)}, f32[8,128]{1,0:T(8,128)S(1)}, u32[]{:S(2)}, u32[]{:S(2)}) %collective-permute-start) | collective-permute-done | bytes 4128 | tf_op jit(solution)/shard_map/ppermute | solution.py:387
  2.8 3.9 %collective-permute-start.2 = (f32[16,128]{1,0:T(8,128)S(1)}, f32[16,128]{1,0:T(8,128)S(1)}, u32[]{:S(2)}, u32[]{:S(2)}) collective-permute-start(f32[16,128]{1,0:T(8,128)S(1)} %pad_maximum_fusion.refs_3_), channel_id=1, source_target_pairs={{0,16},{4,28},{8,24},{12,20},{16,0},{20,12},{24,8},{28,4},{1,17},{... | collective-permute-start | bytes 24584 | tf_op jit(solution)/shard_map/ppermute | solution.py:387
  6.7 1.6 %collective-permute-start.1 = (f32[16,128]{1,0:T(8,128)S(1)}, f32[16,128]{1,0:T(8,128)S(1)}, u32[]{:S(2)}, u32[]{:S(2)}) collective-permute-start(f32[16,128]{1,0:T(8,128)S(1)} %pad_maximum_fusion.refs_3_), channel_id=1, source_target_pairs={{0,8},{4,12},{8,0},{12,4},{16,24},{20,28},{24,16},{28,20},{1,9},{5... | collective-permute-start | bytes 24584 | tf_op jit(solution)/shard_map/ppermute | solution.py:387
  8.3 2.0 %prepare.1 = (f32[16,24,128]{2,1,0:T(8,128)S(1)}, bf16[1024,128]{1,0:T(8,128)(2,1)S(1)}, s32[16,128]{1,0:T(8,128)S(1)}, f32[16,128]{1,0:T(8,128)S(1)}, s32[8,128...) custom-call(s32[2,12]{1,0:T(2,128)} %bitcast.17, f32[24,128]{1,0:T(8,128)} %flow_hbm.3, ...), custom_call_target="tpu_custom_call" | custom-call | tf_op jit(solution)/shard_map/prepare/pallas_call | solution.py:366
  10.3 0.0 collective-permute-done.2.refs_0_
  10.3 0.0 collective-permute-done.1.refs_2_
  10.4 0.0 collective-permute-start.3
  11.1 0.5 %collective-permute-done.3.refs_1_ = f32[16,128]{1,0:T(8,128)S(1)} collective-permute-done((f32[16,128]{1,0:T(8,128)S(1)}, f32[16,128]{1,0:T(8,128)S(1)}, u32[]{:S(2)}, u32[]{:S(2)}) %collective-permute-start.3) | collective-permute-done | bytes 8224 | tf_op jit(solution)/shard_map/ppermute | solution.py:387
  11.6 0.5 %forward.1.part_ref = f32[8,128]{1,0:T(8,128)S(1)} custom-call(s32[2,12]{1,0:T(2,128)S(4)} %get-tuple-element.18.pairs_ref, s32[1,1]{1,0:T(1,128)S(6)} %copy.12.count_ref, s32[16,128]{1,0:T(8,128)S(1)} %get-tuple-element.23.ints_ref, f32[16,128]{1,0:T(8,128)S(1)} %get-tuple-element.20.floats_ref, bf16[12,8,128,128]{3,2,1,0:T(8,128)(2,1)S(1)} %get-tuple-element.24.tile_ref, ...), custom_call_target="tpu_custom_call" | custom-call | tf_op jit(solution)/shard_map/forward/pallas_call | solution.py:366
  12.1 0.2 collective-permute-start.4
  12.3 0.3 turn.1.tile_ref
  12.6 0.7 %collective-permute-done.4 = f32[8,128]{1,0:T(8,128)S(1)} collective-permute-done((f32[8,128]{1,0:T(8,128)S(1)}, f32[8,128]{1,0:T(8,128)S(1)}, u32[]{:S(2)}, u32[]{:S(2)}) %collective-permute-start.4) | collective-permute-done | bytes 4128 | tf_op jit(solution)/shard_map/ppermute | solution.py:387
  13.3 0.9 %collective-permute-start.5 = (f32[8,128]{1,0:T(8,128)S(1)}, f32[8,128]{1,0:T(8,128)S(1)}, u32[]{:S(2)}, u32[]{:S(2)}) collective-permute-start(f32[8,128]{1,0:T(8,128)S(1)} %add.3.refs_3_), channel_id=1, source_target_pairs={{0,16},{4,28},{8,24},{12,20},{16,0},{20,12},{24,8},{28,4},{1,17},{... | collective-permute-start | bytes 12296 | tf_op jit(solution)/shard_map/ppermute | solution.py:387
  14.2 1.7 %collective-permute-start.7 = (f32[8,128]{1,0:T(8,128)S(1)}, f32[8,128]{1,0:T(8,128)S(1)}, u32[]{:S(2)}, u32[]{:S(2)}) collective-permute-start(f32[8,128]{1,0:T(8,128)S(1)} %add.3.refs_3_), channel_id=1, source_target_pairs={{0,8},{4,12},{8,0},{12,4},{16,24},{20,28},{24,16},{28,20},{1,9},{5... | collective-permute-start | bytes 12296 | tf_op jit(solution)/shard_map/ppermute | solution.py:387
  15.9 1.9 %collective-permute-done.5.refs_0_ = f32[8,128]{1,0:T(8,128)S(1)} collective-permute-done((f32[8,128]{1,0:T(8,128)S(1)}, f32[8,128]{1,0:T(8,128)S(1)}, u32[]{:S(2)}, u32[]{:S(2)}) %collective-permute-start.5) | collective-permute-done | bytes 4128 | tf_op jit(solution)/shard_map/ppermute | solution.py:387
  17.8 0.0 collective-permute-start.6
  17.8 0.0 collective-permute-done.7.refs_2_
  17.8 1.2 %collective-permute-done.6.refs_1_ = f32[8,128]{1,0:T(8,128)S(1)} collective-permute-done((f32[8,128]{1,0:T(8,128)S(1)}, f32[8,128]{1,0:T(8,128)S(1)}, u32[]{:S(2)}, u32[]{:S(2)}) %collective-permute-start.6) | collective-permute-done | bytes 4128 | tf_op jit(solution)/shard_map/ppermute | solution.py:387
  19.0 0.7 %backward.1 = f32[128,128]{1,0:T(8,128)S(1)} custom-call(s32[2,12]{1,0:T(2,128)S(4)} %get-tuple-element.18.pairs_ref, s32[1,1]{1,0:T(1,128)S(6)} %copy.12.count_ref, s32[8,128]{1,0:T(8,128)S(1)} %get-tuple-element.19.people_ref, f32[16,128]{1,0:T(8,128)S(1)} %get-tuple-element.20.floats_ref, bf16[1024,128]{1,0:T(8,128)(2,1)S(1)} %get-tuple-element.21.spread_ref, ...), custom_call_target="tpu_custom_call" | custom-call | tf_op jit(solution)/shard_map/backward/pallas_call | solution.py:366
  19.7 11.3 %all_to_all.5 = f32[32,4,128]{2,1,0:T(4,128)S(1)} all-to-all(f32[32,4,128]{2,1,0:T(4,128)S(1)} %bitcast.10), channel_id=1, replica_groups=mesh['src'=8,'rcv'=4] {'rcv','src'}, dimensions={0} | all-to-all | bytes 131072 | tf_op jit(solution)/shard_map/all_to_all | solution.py:509
  31.0 0.9 %finish.1 = (f32[24,128]{1,0:T(8,128)}, f32[24,128]{1,0:T(8,128)}, f32[1,128]{1,0:T(1,128)}) custom-call(f32[128,128]{1,0:T(8,128)S(1)} %bitcast.11, f32[16,24,128]{2,1,0:T(8,128)S(1)} %get-tuple-element.29.table_ref), custom_call_target="tpu_custom_call" | custom-call | tf_op jit(solution)/shard_map/finish/pallas_call | solution.py:366
  (2 shorter events, 0.0 us)
Async XLA Ops:
  1.4 1.3 %collective-permute-start = (f32[8,128]{1,0:T(8,128)S(1)}, f32[8,128]{1,0:T(8,128)S(1)}, u32[]{:S(2)}, u32[]{:S(2)}) collective-permute-start(f32[8,128]{1,0:T(8,128)S(1)} %source.1), channel_id=1, source_target_pairs={{0,4},{4,0},{8,12},{12,8},{16,20},{20,16},{24,28},{28,24},{1,5},{5... | collective-permute-start | bytes 12296 | tf_op jit(solution)/shard_map/ppermute | solution.py:387
  2.8 7.5 %collective-permute-start.2 = (f32[16,128]{1,0:T(8,128)S(1)}, f32[16,128]{1,0:T(8,128)S(1)}, u32[]{:S(2)}, u32[]{:S(2)}) collective-permute-start(f32[16,128]{1,0:T(8,128)S(1)} %pad_maximum_fusion.refs_3_), channel_id=1, source_target_pairs={{0,16},{4,28},{8,24},{12,20},{16,0},{20,12},{24,8},{28,4},{1,17},{... | collective-permute-start | bytes 24584 | tf_op jit(solution)/shard_map/ppermute | solution.py:387
  6.7 3.7 %collective-permute-start.1 = (f32[16,128]{1,0:T(8,128)S(1)}, f32[16,128]{1,0:T(8,128)S(1)}, u32[]{:S(2)}, u32[]{:S(2)}) collective-permute-start(f32[16,128]{1,0:T(8,128)S(1)} %pad_maximum_fusion.refs_3_), channel_id=1, source_target_pairs={{0,8},{4,12},{8,0},{12,4},{16,24},{20,28},{24,16},{28,20},{1,9},{5... | collective-permute-start | bytes 24584 | tf_op jit(solution)/shard_map/ppermute | solution.py:387
  10.4 1.2 %collective-permute-start.3 = (f32[16,128]{1,0:T(8,128)S(1)}, f32[16,128]{1,0:T(8,128)S(1)}, u32[]{:S(2)}, u32[]{:S(2)}) collective-permute-start(f32[16,128]{1,0:T(8,128)S(1)} %collective-permute-done.2.refs_0_), channel_id=1, source_target_pairs={{0,4},{4,0},{8,12},{12,8},{16,20},{20,16},{24,28},{28,24},{1,5},{5... | collective-permute-start | bytes 24584 | tf_op jit(solution)/shard_map/ppermute | solution.py:387
  12.1 1.2 %collective-permute-start.4 = (f32[8,128]{1,0:T(8,128)S(1)}, f32[8,128]{1,0:T(8,128)S(1)}, u32[]{:S(2)}, u32[]{:S(2)}) collective-permute-start(f32[8,128]{1,0:T(8,128)S(1)} %forward.1.part_ref), channel_id=1, source_target_pairs={{0,4},{4,0},{8,12},{12,8},{16,20},{20,16},{24,28},{28,24},{1,5},{5... | collective-permute-start | bytes 12296 | tf_op jit(solution)/shard_map/ppermute | solution.py:387
  13.3 4.5 %collective-permute-start.5 = (f32[8,128]{1,0:T(8,128)S(1)}, f32[8,128]{1,0:T(8,128)S(1)}, u32[]{:S(2)}, u32[]{:S(2)}) collective-permute-start(f32[8,128]{1,0:T(8,128)S(1)} %add.3.refs_3_), channel_id=1, source_target_pairs={{0,16},{4,28},{8,24},{12,20},{16,0},{20,12},{24,8},{28,4},{1,17},{... | collective-permute-start | bytes 12296 | tf_op jit(solution)/shard_map/ppermute | solution.py:387
  14.2 3.7 %collective-permute-start.7 = (f32[8,128]{1,0:T(8,128)S(1)}, f32[8,128]{1,0:T(8,128)S(1)}, u32[]{:S(2)}, u32[]{:S(2)}) collective-permute-start(f32[8,128]{1,0:T(8,128)S(1)} %add.3.refs_3_), channel_id=1, source_target_pairs={{0,8},{4,12},{8,0},{12,4},{16,24},{20,28},{24,16},{28,20},{1,9},{5... | collective-permute-start | bytes 12296 | tf_op jit(solution)/shard_map/ppermute | solution.py:387
  17.8 1.2 %collective-permute-start.6 = (f32[8,128]{1,0:T(8,128)S(1)}, f32[8,128]{1,0:T(8,128)S(1)}, u32[]{:S(2)}, u32[]{:S(2)}) collective-permute-start(f32[8,128]{1,0:T(8,128)S(1)} %collective-permute-done.5.refs_0_), channel_id=1, source_target_pairs={{0,4},{4,0},{8,12},{12,8},{16,20},{20,16},{24,28},{28,24},{1,5},{5... | collective-permute-start | bytes 12296 | tf_op jit(solution)/shard_map/ppermute | solution.py:387
